TPU v7x, 32 devices: a whole 2x2x4 slice. The times are simulated.
32 devices in a mesh: seq: 8 (over z, y), rows: 4 (over x, core).
Axes of the slice: x: 2, y: 2, z: 4, core: 2. Of those that a mesh axis runs over, the one named last changes fastest.
Arguments:
- tokens: bfloat16 [64, 1024, 512], P('rows', 'seq'), may hold values from -8 to 8
- cotangent: bfloat16 [64, 1024, 512], P('rows', 'seq'), may hold values from -6 to 6
- reset_pos: int32 [64, 8], P('rows'), may hold values from 0 to 1023, as said below
- norm1_gain: float32 [512], replicated, may hold values from 0.1 to 1.9
- w_in: bfloat16 [512, 3072], replicated, may hold values from -0.25 to 0.25
- forget_bias: float32 [1024], replicated, may hold values from 0.5 to 1.5
- input_bias: float32 [1024], replicated, may hold values from -14 to -3
- w_out: bfloat16 [1024, 512], replicated, may hold values from -0.75 to 0.75
- norm2_gain: float32 [512], replicated, may hold values from 0.1 to 1.9
- w_up: bfloat16 [512, 2048], replicated, may hold values from -0.25 to 0.25
- up_bias: float32 [2048], replicated, may hold values from -3 to 3
- w_down: bfloat16 [2048, 512], replicated, may hold values from -0.125 to 0.125
- down_bias: float32 [512], replicated, may hold values from -3 to 3
Outputs:
- mixed: bfloat16 [64, 1024, 512], P('rows', 'seq')
- grad_tokens: float32 [64, 1024, 512], P('rows', 'seq')
- grad_norm1_gain: float32 [512], replicated
- grad_w_in: float32 [512, 3072], replicated
- grad_forget_bias: float32 [1024], replicated
- grad_input_bias: float32 [1024], replicated
- grad_w_out: float32 [1024, 512], replicated
- grad_norm2_gain: float32 [512], replicated
- grad_w_up: float32 [512, 2048], replicated
- grad_up_bias: float32 [2048], replicated
- grad_w_down: float32 [2048, 512], replicated
- grad_down_bias: float32 [512], replicated
Inputs may be any that keep to these rules, and one draw needn't show every extreme that they name: `reset_pos`: 0 marks no start. In each aligned block of 16 rows, one row, drawn from the seed, holds only zeros.
All inputs are finite; a program needn't handle non-finite values.
Results may differ from a plain program's by a relative error of at most 0.0062.
Values sent between devices are 32-bit elements; how exact they have to be, the bound alone decides.
A program may use at most 256 MiB of HBM per device.

v0:
```python
import math

import jax
import jax.numpy as jnp
from jax import lax
from jax.sharding import PartitionSpec as P


def carried_in(part, axis, combine, identity, reverse):
    count = lax.axis_size(axis)
    place = lax.axis_index(axis)
    ahead = count - 1 - place if reverse else place
    gathered = jax.tree.map(lambda a: lax.all_gather(a, axis), part)
    state = jax.tree.map(lambda a, e: jnp.zeros_like(a) + jnp.asarray(e, a.dtype), part, identity)

    def one(hop, state):
        source = count - 1 - hop if reverse else hop
        return combine(
            state, jax.tree.map(lambda a: lax.dynamic_index_in_dim(a, source, 0, False), gathered)
        )

    return lax.fori_loop(0, ahead, one, state)


def root_norm(values, gain):
    return values * lax.rsqrt(jnp.mean(values * values, axis=-1, keepdims=True) + 1e-06) * gain


def gate_terms(part_forget, part_input, part_cand, bias_forget, bias_input):
    log_forget = -jax.nn.softplus(-(part_forget + bias_forget))
    log_input = -jax.nn.softplus(-(part_input + bias_input))
    log_total = jnp.logaddexp(log_forget, log_input)
    return (jnp.exp(log_forget - log_total), jnp.exp(log_input - log_total) * part_cand)


def affine_join(earlier, later):
    return (earlier[0] * later[0], later[0] * earlier[1] + later[1])


def left_dot(left, right):
    return lax.dot_general(
        left, right, (((0,), (0,)), ((), ())), preferred_element_type=jnp.float32
    )


def right_dot(left, right):
    return lax.dot_general(
        left, right, (((1,), (1,)), ((), ())), preferred_element_type=jnp.float32
    )


def shift_gelu(values, shift):
    return jax.nn.gelu(values + shift)


def on_device(
    tokens,
    cotangent,
    reset_pos,
    norm1_gain,
    w_in,
    forget_bias,
    input_bias,
    w_out,
    norm2_gain,
    w_up,
    up_bias,
    w_down,
    down_bias,
):
    row_count, steps_dev, width = tokens.shape
    hidden = w_out.shape[0]
    total = row_count * steps_dev
    inner = math.gcd(steps_dev, max(1, steps_dev // 16))
    turns = steps_dev // inner
    inputs = tokens.reshape(total, width).astype(jnp.float32)
    places = lax.axis_index("seq") * steps_dev + jnp.arange(steps_dev, dtype=jnp.int32)
    starts = jnp.any(reset_pos[:, :, None] == places[None, None, :], axis=1)
    kept = jnp.where(starts, 0.0, 1.0).astype(jnp.float32)
    kept_time = jnp.transpose(kept)[:, :, None]
    w_forget = w_in[:, :hidden]
    w_input = w_in[:, hidden : 2 * hidden]
    w_cand = w_in[:, 2 * hidden :]
    normed, norm1_pull = jax.vjp(root_norm, inputs, norm1_gain)
    normed_low = normed.astype(jnp.bfloat16)
    part_forget = jnp.dot(normed_low, w_forget, preferred_element_type=jnp.float32)
    part_input = jnp.dot(normed_low, w_input, preferred_element_type=jnp.float32)
    part_cand = jnp.dot(normed_low, w_cand, preferred_element_type=jnp.float32)
    (decay_raw, update), gate_pull = jax.vjp(
        gate_terms, part_forget, part_input, part_cand, forget_bias, input_bias
    )
    decay_time = jnp.moveaxis(decay_raw.reshape(row_count, steps_dev, hidden), 1, 0) * kept_time
    update_time = jnp.moveaxis(update.reshape(row_count, steps_dev, hidden), 1, 0)
    decay_blocks = decay_time.reshape(turns, inner, row_count, hidden)
    update_blocks = update_time.reshape(turns, inner, row_count, hidden)
    ones_rows = jnp.ones((row_count, hidden), jnp.float32)
    zero_rows = jnp.zeros((row_count, hidden), jnp.float32)

    def summary_step(carry, pieces):
        product, running = carry
        decay_piece, update_piece = pieces
        for offset in range(inner):
            running = decay_piece[offset] * running + update_piece[offset]
            product = decay_piece[offset] * product
        return ((product, running), None)

    (local_product, local_end), unused = lax.scan(
        summary_step, (ones_rows, zero_rows), (decay_blocks, update_blocks)
    )
    carried = carried_in(
        (local_product, local_end), "seq", affine_join, (ones_rows, zero_rows), False
    )[1]

    def state_step(running, pieces):
        decay_piece, update_piece = pieces
        states_out = []
        before_out = []
        for offset in range(inner):
            before_out.append(running)
            running = decay_piece[offset] * running + update_piece[offset]
            states_out.append(running)
        return (running, (jnp.stack(states_out), jnp.stack(before_out)))

    unused_end, (state_blocks, before_blocks) = lax.scan(
        state_step, carried, (decay_blocks, update_blocks)
    )
    state_time = state_blocks.reshape(steps_dev, row_count, hidden)
    before_time = before_blocks.reshape(steps_dev, row_count, hidden)
    state_low = jnp.moveaxis(state_time.astype(jnp.bfloat16), 0, 1).reshape(total, hidden)
    middle = inputs + jnp.dot(state_low, w_out, preferred_element_type=jnp.float32)
    normed_two, norm2_pull = jax.vjp(root_norm, middle, norm2_gain)
    normed_two_low = normed_two.astype(jnp.bfloat16)
    up_pre = jnp.dot(normed_two_low, w_up, preferred_element_type=jnp.float32)
    activated, gelu_pull = jax.vjp(shift_gelu, up_pre, up_bias)
    activated_low = activated.astype(jnp.bfloat16)
    result = middle + jnp.dot(activated_low, w_down, preferred_element_type=jnp.float32) + down_bias
    mixed = result.astype(jnp.bfloat16).reshape(row_count, steps_dev, width)
    back_out = cotangent.reshape(total, width)
    grad_down = left_dot(activated_low, back_out)
    grad_down_bias = jnp.sum(back_out.astype(jnp.float32), axis=0)
    back_act = right_dot(back_out, w_down)
    back_up, grad_up_bias = gelu_pull(back_act)
    back_up_low = back_up.astype(jnp.bfloat16)
    grad_up = left_dot(normed_two_low, back_up_low)
    back_norm_two = right_dot(back_up_low, w_up)
    back_mid_norm, grad_norm2 = norm2_pull(back_norm_two)
    back_middle = back_out.astype(jnp.float32) + back_mid_norm
    back_mid_low = back_middle.astype(jnp.bfloat16)
    grad_out = left_dot(state_low, back_mid_low)
    back_state = right_dot(back_mid_low, w_out).reshape(row_count, steps_dev, hidden)
    back_state_blocks = jnp.moveaxis(back_state, 1, 0).reshape(turns, inner, row_count, hidden)

    def back_summary(carry, pieces):
        product, flowing = carry
        decay_piece, back_piece = pieces
        for offset in reversed(range(inner)):
            flowing = decay_piece[offset] * (back_piece[offset] + flowing)
            product = decay_piece[offset] * product
        return ((product, flowing), None)

    (back_product, back_end), unused = lax.scan(
        back_summary, (ones_rows, zero_rows), (decay_blocks, back_state_blocks), reverse=True
    )
    returned = carried_in(
        (back_product, back_end), "seq", affine_join, (ones_rows, zero_rows), True
    )[1]

    def back_step(flowing, pieces):
        decay_piece, back_piece = pieces
        totals_out = [None] * inner
        for offset in reversed(range(inner)):
            total_here = back_piece[offset] + flowing
            totals_out[offset] = total_here
            flowing = decay_piece[offset] * total_here
        return (flowing, jnp.stack(totals_out))

    unused_flow, total_blocks = lax.scan(
        back_step, returned, (decay_blocks, back_state_blocks), reverse=True
    )
    back_total_time = total_blocks.reshape(steps_dev, row_count, hidden)
    back_decay_time = back_total_time * before_time * kept_time
    back_decay = jnp.moveaxis(back_decay_time, 0, 1).reshape(total, hidden)
    back_total = jnp.moveaxis(back_total_time, 0, 1).reshape(total, hidden)
    back_forget, back_input, back_cand, grad_forget, grad_input = gate_pull(
        (back_decay, back_total)
    )
    forget_low = back_forget.astype(jnp.bfloat16)
    input_low = back_input.astype(jnp.bfloat16)
    cand_low = back_cand.astype(jnp.bfloat16)
    grad_in = jnp.concatenate(
        [
            left_dot(normed_low, forget_low),
            left_dot(normed_low, input_low),
            left_dot(normed_low, cand_low),
        ],
        axis=1,
    )
    back_norm_one = (
        right_dot(forget_low, w_forget)
        + right_dot(input_low, w_input)
        + right_dot(cand_low, w_cand)
    )
    back_in_norm, grad_norm1 = norm1_pull(back_norm_one)
    back_inputs = (back_middle + back_in_norm).reshape(row_count, steps_dev, width)
    (
        grad_norm1,
        grad_in,
        grad_forget,
        grad_input,
        grad_out,
        grad_norm2,
        grad_up,
        grad_up_bias,
        grad_down,
        grad_down_bias,
    ) = lax.psum(
        (
            grad_norm1,
            grad_in,
            grad_forget,
            grad_input,
            grad_out,
            grad_norm2,
            grad_up,
            grad_up_bias,
            grad_down,
            grad_down_bias,
        ),
        ("seq", "rows"),
    )
    return (
        mixed,
        back_inputs,
        grad_norm1,
        grad_in,
        grad_forget,
        grad_input,
        grad_out,
        grad_norm2,
        grad_up,
        grad_up_bias,
        grad_down,
        grad_down_bias,
    )


def solution(mesh):
    return jax.shard_map(
        on_device,
        mesh=mesh,
        in_specs=(
            P("rows", "seq", None),
            P("rows", "seq", None),
            P("rows", None),
            P(),
            P(),
            P(),
            P(),
            P(),
            P(),
            P(),
            P(),
            P(),
            P(),
        ),
        out_specs=(
            P("rows", "seq", None),
            P("rows", "seq", None),
            P(),
            P(),
            P(),
            P(),
            P(),
            P(),
            P(),
            P(),
            P(),
            P(),
        ),
        check_vma=False,
    )
```

profile of v0, /device:TPU:0, one launch (start us, length us, event | category | flops | bytes accessed | tf_op | source)
XLA Modules:
  0.0 909.5 jit_solution(12453162844632757065)
XLA Ops:
  26.2 29.0 %fusion.138 = (f32[2048,1024]{1,0:T(8,128)}, f32[2048,1024]{1,0:T(8,128)}, f32[2048,1024]{1,0:T(8,128)}) fusion(f32[2048,1024]{1,0:T(8,128)} %fusion.128, f32[1024]{0:T(1024)S(1)} %copy-done.30, f32[2048,1024]{1,0:T(8,128)} %fusion.131, f32[1024]{0:T(1024)S(1)} %copy-done.32, bf16[2048,512]{1,0:T(8,128)(2,1)} %copy-done.20, bf16[512,3072]{1,0:T(8,128)(2,1)} %param.30), kind=kOutput, calls=%fused_computation.284 | convolution fusion | flops 2208301056 | bytes 45096960 | tf_op jit(solution)/shard_map/dot_general | solution.py:88
  55.3 11.6 %copy.42 = f32[128,16,1024]{2,1,0:T(8,128)} copy(f32[128,16,1024]{2,0,1:T(8,128)} %bitcast.702) | data formatting | bytes 16777216 | tf_op jit(solution)/shard_map/transpose | solution.py:93
  67.5 8.1 copy.41
  75.6 21.7 %while.90 = (s32[]{:T(128)}, f32[16,1024]{1,0:T(8,128)S(1)}, f32[16,1024]{1,0:T(8,128)S(1)}, f32[16,8,16,1024]{3,2,1,0:T(8,128)}, f32[16,8,16,1024]{3,2,1,0:T(8,...) while((s32[]{:T(128)}, f32[16,1024]{1,0:T(8,128)S(1)}, ...), condition=%wide.region_3.5_spmd.clone, body=%wide.region_2.4_spmd.clone.sunk | while | flops 425994 | bytes 1310987 | solution.py:107
  97.3 33.0 %all-gather.1 = f32[128,1024]{1,0:T(8,128)S(1)} all-gather(f32[16,1024]{1,0:T(8,128)S(1)} %get-tuple-element.415), channel_id=3, replica_groups=mesh['seq'=8,'rows'=4] {'seq'}, dimensions={0}, use_global_device_ids=true | all-gather | bytes 589824 | tf_op jit(solution)/shard_map/all_gather | solution.py:13
  130.3 31.3 %all-gather = f32[128,1024]{1,0:T(8,128)S(1)} all-gather(f32[16,1024]{1,0:T(8,128)S(1)} %get-tuple-element.414), channel_id=2, replica_groups=mesh['seq'=8,'rows'=4] {'seq'}, dimensions={0}, use_global_device_ids=true | all-gather | bytes 589824 | tf_op jit(solution)/shard_map/all_gather | solution.py:13
  165.9 140.5 %while.87 = (s32[]{:T(128)}, f32[16,1024]{1,0:T(8,128)S(1)}, bf16[16,8,16,1024]{3,2,1,0:T(8,128)(2,1)}, f32[16,8,16,1024]{3,2,1,0:T(8,128)}, f32[16,8,16,1024]{3...) while((s32[]{:T(128)}, f32[16,1024]{1,0:T(8,128)S(1)}, ...), condition=%wide.region_7.9_spmd, body=%wide.region_6.8_spmd.sunk | while | flops 262152 | bytes 4849965 | solution.py:124
  313.9 12.4 %multiply_convert_fusion = (bf16[2048,2048]{1,0:T(8,128)(2,1)}, f32[2048,2048]{1,0:T(8,128)}) fusion(f32[2048]{0:T(1024)S(1)} %copy-done.37, bf16[512,2048]{1,0:T(8,128)(2,1)S(1)} %copy-done, f32[2048,512]{1,0:T(8,128)S(1)} %get-tuple-element.584, f32[512]{0:T(512)S(1)} %copy-done.35, f32[2048]{0:T(1024)S(1)} %fusion.136), kind=kOutput, calls=%fused_computation.192 | convolution fusion | flops 4340056064 | bytes 31475712 | tf_op jit(solution)/shard_map/dot_general | solution.py:133
  326.4 18.5 %fusion.158 = (f32[2048]{0:T(1024)S(1)}, bf16[2048,2048]{1,0:T(8,128)(2,1)}) fusion(f32[2048,2048]{1,0:T(8,128)} %get-tuple-element.586, f32[2048]{0:T(1024)S(1)} %copy-done.37, bf16[2048,512]{1,0:T(8,128)(2,1)S(1)} %bitcast.700, bf16[2048,512]{1,0:T(8,128)(2,1)} %param.37), kind=kOutput, calls=%fused_computation.287 | convolution fusion | flops 4387239936 | bytes 29376512 | tf_op jit(solution)/shard_map/dot_general | solution.py:47
  344.9 10.3 %fusion.112 = f32[512,2048]{1,0:T(8,128)} fusion(bf16[2048,2048]{1,0:T(8,128)(2,1)} %get-tuple-element.590, f32[2048,512]{1,0:T(8,128)S(1)} %get-tuple-element.584, f32[512]{0:T(512)S(1)} %copy-done.35, f32[2048]{0:T(1024)S(1)} %fusion.136), kind=kOutput, calls=%fused_computation.246 | convolution fusion | flops 4298113024 | bytes 16787456 | tf_op jit(solution)/shard_map/dot_general | solution.py:41
  371.7 10.1 %fusion.160 = f32[2048,512]{1,0:T(8,128)} fusion(bf16[2048,2048]{1,0:T(8,128)(2,1)} %get-tuple-element.585, bf16[2048,512]{1,0:T(8,128)(2,1)S(1)} %bitcast.701), kind=kOutput, calls=%fused_computation.290 | convolution fusion | flops 4294967296 | bytes 14680064 | tf_op jit(solution)/shard_map/dot_general | solution.py:41
  381.8 8.1 copy.44
  389.9 21.7 %while.91 = (s32[]{:T(128)}, f32[16,1024]{1,0:T(8,128)S(1)}, f32[16,1024]{1,0:T(8,128)S(1)}, f32[16,8,16,1024]{3,2,1,0:T(8,128)}, f32[16,8,16,1024]{3,2,1,0:T(8,...) while((s32[]{:T(128)}, f32[16,1024]{1,0:T(8,128)S(1)}, ...), condition=%wide.region_11.13_spmd.clone, body=%wide.region_10.12_spmd.clone.sunk | while | flops 425995 | bytes 1311007 | solution.py:161
  411.6 31.6 %all-gather.3 = f32[128,1024]{1,0:T(8,128)S(1)} all-gather(f32[16,1024]{1,0:T(8,128)S(1)} %get-tuple-element.419), channel_id=5, replica_groups=mesh['seq'=8,'rows'=4] {'seq'}, dimensions={0}, use_global_device_ids=true | all-gather | bytes 589824 | tf_op jit(solution)/shard_map/all_gather | solution.py:13
  443.2 31.5 %all-gather.2 = f32[128,1024]{1,0:T(8,128)S(1)} all-gather(f32[16,1024]{1,0:T(8,128)S(1)} %get-tuple-element.418), channel_id=4, replica_groups=mesh['seq'=8,'rows'=4] {'seq'}, dimensions={0}, use_global_device_ids=true | all-gather | bytes 589824 | tf_op jit(solution)/shard_map/all_gather | solution.py:13
  479.3 63.2 %while.89 = (s32[]{:T(128)}, f32[16,1024]{1,0:T(8,128)S(1)}, f32[16,8,16,1024]{3,2,1,0:T(8,128)}, f32[16,8,16,1024]{3,2,1,0:T(8,128)}, f32[16,8,16,1024]{3,2,1,0...) while((s32[]{:T(128)}, f32[16,1024]{1,0:T(8,128)S(1)}, ...), condition=%wide.region_15.17_spmd, body=%wide.region_14.16_spmd.sunk | while | flops 278537 | bytes 3801373 | solution.py:177
  542.5 17.4 %fusion.101 = (f32[128,16,1024]{2,0,1:T(8,128)S(1)}, f32[128,16,1024]{2,0,1:T(8,128)S(1)}) fusion(f32[128,16,1024]{2,1,0:T(8,128)} %bitcast.694, f32[128,16]{0,1:T(8,128)S(1)} %select_bitcast_fusion, f32[128,16,1024]{2,1,0:T(8,128)} %bitcast.695), kind=kLoop, calls=%fused_computation.215 | loop fusion | flops 4194304 | bytes 33562624 | tf_op jit(solution)/shard_map/mul | solution.py:181
  560.0 33.7 %fusion.154 = (f32[1024]{0:T(1024)S(1)}, f32[2048,1024]{1,0:T(8,128)}, f32[1024]{0:T(1024)S(1)}, f32[2048,1024]{1,0:T(8,128)}, bf16[2048,1024]{1,0:T(8,128)(2,1)}) fusion(f32[128,16,1024]{2,0,1:T(8,128)S(1)} %get-tuple-element.580, f32[2048,1024]{1,0:T(8,128)} %fusion.131, f32[1024]{0:T(1024)S(1)} %copy-done.33, f32[2048,1024]{1,0:T(8,128)} %fusion.128, ...), kind=kLoop, calls=%fused_computation.285 | loop fusion | flops 134215680 | bytes 62930944 | tf_op jit(solution)/shard_map/transpose(jvp())/reduce_sum | solution.py:31
  593.7 5.9 fusion.118
  609.4 6.3 fusion.119
  625.5 41.6 %all-reduce = (f32[512]{0:T(512)}, f32[1024]{0:T(1024)}, f32[1024]{0:T(1024)}, f32[512]{0:T(512)}, f32[2048]{0:T(1024)}, /*index=5*/f32[512]{0:T(512)}) all-reduce(f32[512]{0:T(512)S(1)} %get-tuple-element.463, f32[1024]{0:T(1024)S(1)} %neg.51, f32[1024]{0:T(1024)S(1)} %neg.52, ...), channel_id=1, replica_groups=mesh['seq'=8,'rows'=4] {'seq','rows'}, use_global_device_ids=true, to_apply=%region_18.20 | all-reduce | flops 5632 | bytes 45056 | tf_op jit(solution)/shard_map/psum | solution.py:216
  674.3 9.4 %add_convert_fusion = bf16[2048,512]{1,0:T(8,128)(2,1)} fusion(f32[2048,512]{1,0:T(8,128)S(1)} %copy-done.14, bf16[2048,2048]{1,0:T(8,128)(2,1)} %get-tuple-element.585, bf16[2048,512]{1,0:T(8,128)(2,1)S(1)} %copy-done.36, f32[512]{0:T(512)S(1)} %copy-done.38), kind=kOutput, calls=%fused_computation.250 | convolution fusion | flops 4298113024 | bytes 16779264 | tf_op jit(solution)/shard_map/dot_general | solution.py:136
  683.7 205.9 %all-reduce.4.cloned.1.call-done = (f32[512,3072]{1,0:T(8,128)}, f32[1024,512]{1,0:T(8,128)}, f32[512,2048]{1,0:T(8,128)}, f32[2048,512]{1,0:T(8,128)}) async-done(((f32[512,3072]{1,0:T(8,128)}, f32[1024,512]{1,0:T(8,128)}, f32[512,2048]{1,0:T(8,128)}, f32[2048,512]{1,0:T(8,128)}), (f32[512,3072]{1,0:T(8,128)}, f32[1024,512]{1,0:T(8,128)}, f32[512,2048]{1,0:T(8,128)}, ...) | async-done | bytes 16777232 | tf_op jit(solution)/shard_map/psum | solution.py:216
  889.6 6.4 copy.132
  (520 shorter events, 330.6 us)
Async XLA Ops:
  7.2 306.7 %copy-start = (bf16[512,2048]{1,0:T(8,128)(2,1)S(1)}, bf16[512,2048]{1,0:T(8,128)(2,1)}, u32[]{:S(2)}) copy-start(bf16[512,2048]{1,0:T(8,128)(2,1)} %param.35) | copy-start | bytes 6291460
  7.2 882.4 %all-reduce.4.cloned.1.call-start = ((), (), s32[]{:S(2)}) async-start(), calls=%async_computation | async-start | bytes 33554432 | tf_op jit(solution)/shard_map/psum | solution.py:216
  7.3 7.2 copy-start.23
  12.3 8.0 copy-start.27
  12.3 7.9 copy-start.25
  55.2 11.6 %copy-start.12 = (f32[2048,1024]{1,0:T(8,128)S(1)}, f32[2048,1024]{1,0:T(8,128)}, u32[]{:S(2)}) copy-start(f32[2048,1024]{1,0:T(8,128)} %get-tuple-element.579) | copy-start | bytes 25165828
  313.8 47.1 %copy-start.13 = (f32[2048,512]{1,0:T(8,128)}, f32[2048,512]{1,0:T(8,128)S(1)}, u32[]{:S(2)}) copy-start(f32[2048,512]{1,0:T(8,128)S(1)} %get-tuple-element.584) | copy-start | bytes 12582916
  313.9 12.5 %copy-start.9 = (bf16[16,128,512]{2,1,0:T(8,128)(2,1)S(1)}, bf16[16,128,512]{2,1,0:T(8,128)(2,1)}, u32[]{:S(2)}) copy-start(bf16[16,128,512]{2,1,0:T(8,128)(2,1)} %param.27) | copy-start | bytes 6291460
  344.9 10.3 %copy-start.39 = (bf16[2048,2048]{1,0:T(8,128)(2,1)S(1)}, bf16[2048,2048]{1,0:T(8,128)(2,1)}, u32[]{:S(2)}) copy-start(bf16[2048,2048]{1,0:T(8,128)(2,1)} %get-tuple-element.590) | copy-start | bytes 25165828
  371.7 10.1 %copy-start.3 = (f32[2048,1024]{1,0:T(8,128)S(1)}, f32[2048,1024]{1,0:T(8,128)}, u32[]{:S(2)}) copy-start(f32[2048,1024]{1,0:T(8,128)} %fusion.122) | copy-start | bytes 25165828
  381.8 8.1 copy-start.17
  381.8 8.1 copy-start.18
  542.5 17.5 %copy-start.31 = (f32[1024]{0:T(1024)S(1)}, f32[1024]{0:T(1024)}, u32[]{:S(2)}) copy-start(f32[1024]{0:T(1024)} %param.32) | copy-start | bytes 12292
  542.5 17.5 %copy-start.33 = (f32[1024]{0:T(1024)S(1)}, f32[1024]{0:T(1024)}, u32[]{:S(2)}) copy-start(f32[1024]{0:T(1024)} %param.31) | copy-start | bytes 12292
  560.0 33.8 %copy-start.21 = (bf16[2048,512]{1,0:T(8,128)(2,1)S(1)}, bf16[2048,512]{1,0:T(8,128)(2,1)}, u32[]{:S(2)}) copy-start(bf16[2048,512]{1,0:T(8,128)(2,1)} %copy-done.20) | copy-start | bytes 6291460
  609.1 6.6 slice-start
  609.4 7.0 slice-start.1
  609.4 8.0 copy-start.24
  620.3 46.9 %copy-start.28 = (f32[16,128]{1,0:T(8,128)S(1)}, f32[16,128]{1,0:T(8,128)}, u32[]{:S(2)}) copy-start(f32[16,128]{1,0:T(8,128)} %copy-done.27) | copy-start | bytes 24580
  625.5 47.3 %copy-start.38 = (f32[512]{0:T(512)S(1)}, f32[512]{0:T(512)}, u32[]{:S(2)}) copy-start(f32[512]{0:T(512)} %param.38) | copy-start | bytes 6148
  667.1 6.4 copy-start.14
  667.2 7.1 copy-start.36
  889.6 7.7 copy-start.16
  896.0 6.5 copy-start.1
  (19 other events, 79.5 us)
Sparse Core Ops, SparseCore 0:
  607.6 281.9 all-reduce.3
where the time goes:
time: 925 us; the launch traced here: 909 us
  other arithmetic  275 us (30%)
  waiting for transfers between devices  206 us (22%)
  blocking collectives  169 us (18%)
  matrix products  143 us (15%)
  local copies, waits for them, and re-layouts  99 us (11%)
  between operations  14.7 us (2%)
    psum x1, waiting for transfers between devices, on_device(): lax.psum((grad_norm1, grad_in, grad_forget, grad_input, grad_out, grad_no...  206 us
    all_gather x4, blocking collectives, carried_in(): gathered = jax.tree.map(lambda a: lax.all_gather(a, axis), part)  127 us
    while x112, other arithmetic  107 us
    dot_general x6, matrix products, right_dot(): lax.dot_general(left, right, (((1,), (1,)), ((), ())), preferred_element_...  43.7 us
    psum x1, blocking collectives, on_device(): lax.psum((grad_norm1, grad_in, grad_forget, grad_input, grad_out, grad_no...  41.6 us
    dynamic_update_slice x48, local copies, waits for them, and re-layouts, on_device(): lax.scan(state_step, carried, (decay_blocks, update_blocks))  38.7 us
    dot_general x6, matrix products, left_dot(): lax.dot_general(left, right, (((0,), (0,)), ((), ())), preferred_element_...  34.8 us
    reduce_sum x1, other arithmetic, gate_terms(): log_input = -jax.nn.softplus(-(part_input + bias_input))  33.7 us
  transfers between devices with their start and end apart: 1, of which 1 were waited for; matrix products, arithmetic and copies ran while one was open for 3% of the time, Pallas kernels for 0%

commit v1 on v0

--- a/solution.py
+++ b/solution.py
@@ -1,9 +1,277 @@
+import functools
 import math
 
 import jax
 import jax.numpy as jnp
 from jax import lax
+from jax.experimental import pallas as pl
+from jax.experimental.pallas import tpu as pltpu
 from jax.sharding import PartitionSpec as P
+
+MESH = pl.DeviceIdType.MESH
+STAGES = 13
+KINDS = 14
+
+
+def place():
+    seq = lax.axis_index("seq")
+    rows = lax.axis_index("rows")
+    return lax.div(rows, 2), lax.rem(seq, 2), lax.div(seq, 2), lax.rem(rows, 2)
+
+
+def spot(x, y, z, core):
+    return (z * 2 + y, x * 2 + core)
+
+
+def greet(partners):
+    barrier = pltpu.get_barrier_semaphore()
+    x, y, z, core = place()
+    for there in partners:
+        pl.semaphore_signal(barrier, inc=1, device_id=there, device_id_type=MESH)
+
+    @pl.when(z > 0)
+    def _():
+        pl.semaphore_signal(barrier, inc=1, device_id=spot(x, y, z - 1, core), device_id_type=MESH)
+
+    @pl.when(z < 3)
+    def _():
+        pl.semaphore_signal(barrier, inc=1, device_id=spot(x, y, z + 1, core), device_id_type=MESH)
+
+    pl.semaphore_wait(barrier, len(partners) + jnp.where(z > 0, 1, 0) + jnp.where(z < 3, 1, 0))
+
+
+class Summing:
+    def __init__(self, grads, slots, half_in, part_in, up_in, down_in, last_in, result, send, recv, local):
+        self.grads, self.slots = grads, slots
+        self.half_in, self.part_in, self.up_in, self.down_in, self.last_in = half_in, part_in, up_in, down_in, last_in
+        self.result, self.send, self.recv, self.local = result, send, recv, local
+        x, y, z, core = place()
+        self.z = z
+        first = core == 0
+        self.sibling = spot(x, y, z, 1 - core)
+        along_x, along_y = spot(1 - x, y, z, core), spot(x, 1 - y, z, core)
+        self.near = tuple(jnp.where(first, a, b) for a, b in zip(along_x, along_y))
+        self.far = tuple(jnp.where(first, b, a) for a, b in zip(along_x, along_y))
+        self.above = spot(x, y, z + 1, core)
+        self.below = spot(x, y, z - 1, core)
+        near_bit = jnp.where(first, x, y)
+        far_bit = jnp.where(first, y, x)
+        self.half = core * 256
+        self.other_half = (1 - core) * 256
+        self.part = self.half + near_bit * 128
+        self.other_part = self.half + (1 - near_bit) * 128
+        self.far_bit = far_bit
+
+    def copy(self, kind, unit, source, target, device):
+        return pltpu.make_async_remote_copy(
+            src_ref=source, dst_ref=target, send_sem=self.send.at[kind, unit], recv_sem=self.recv.at[kind, unit],
+            device_id=device, device_id_type=MESH,
+        )
+
+    def rows(self, unit, start, count):
+        return self.grads.at[lax.rem(unit, self.slots), pl.ds(pl.multiple_of(start, 8), count)]
+
+    def done(self, unit, start, count):
+        return self.result.at[unit, pl.ds(pl.multiple_of(start, 8), count)]
+
+    def c_half(self, u):
+        return self.copy(0, u, self.rows(u, self.other_half, 256), self.half_in.at[lax.rem(u, 2)], self.sibling)
+
+    def c_part(self, u):
+        return self.copy(1, u, self.rows(u, self.other_part, 128), self.part_in.at[lax.rem(u, 2)], self.near)
+
+    def c_up(self, u, z):
+        lo = 32 * (z + 1)
+        return self.copy(2, u, self.rows(u, self.part + lo, 128 - lo), self.up_in.at[lax.rem(u, 4), pl.ds(lo - 32, 128 - lo)], self.above)
+
+    def c_down(self, u, z):
+        return self.copy(3, u, self.rows(u, self.part, 32 * z), self.down_in.at[lax.rem(u, 4), pl.ds(0, 32 * z)], self.below)
+
+    def c_last(self, u):
+        return self.copy(4, u, self.rows(u, self.part + 32 * self.z + 16 * (1 - self.far_bit), 16), self.last_in.at[u], self.far)
+
+    def c_own(self, u):
+        start = self.part + 32 * self.z + 16 * self.far_bit
+        return pltpu.make_async_copy(self.rows(u, start, 16), self.done(u, start, 16), self.local.at[u])
+
+    def c_far(self, u):
+        start = self.part + 32 * self.z + 16 * self.far_bit
+        return self.copy(5, u, self.rows(u, start, 16), self.done(u, start, 16), self.far)
+
+    def c_rise(self, u, hop):
+        piece = self.done(u, self.part + 32 * (self.z - hop), 32)
+        return self.copy(6 + hop, u, piece, piece, self.above)
+
+    def c_fall(self, u, hop):
+        piece = self.done(u, self.part + 32 * (self.z + hop), 32)
+        return self.copy(9 + hop, u, piece, piece, self.below)
+
+    def c_near(self, u):
+        piece = self.done(u, self.part, 128)
+        return self.copy(12, u, piece, piece, self.near)
+
+    def c_sibling(self, u):
+        piece = self.done(u, self.half, 256)
+        return self.copy(13, u, piece, piece, self.sibling)
+
+    def add(self, u, start, count, ref):
+        here = self.rows(u, start, count)
+        here[...] = here[...] + ref[...]
+
+    def stage(self, s, u):
+        z = self.z
+        if s == 0:
+            self.c_half(u).start()
+        elif s == 1:
+            self.c_half(u).wait()
+            self.add(u, self.half, 256, self.half_in.at[lax.rem(u, 2)])
+            self.c_part(u).start()
+        elif s == 2:
+            self.c_part(u).wait()
+            self.add(u, self.part, 128, self.part_in.at[lax.rem(u, 2)])
+        if 2 <= s <= 5:
+            for k in range(4):
+                if s == 2 + k:
+                    @pl.when(z == k)
+                    def _():
+                        if k > 0:
+                            self.c_up(u, k - 1).wait_recv()
+                            self.add(u, self.part + 32 * k, 128 - 32 * k, self.up_in.at[lax.rem(u, 4), pl.ds(32 * k - 32, 128 - 32 * k)])
+                        if k < 3:
+                            self.c_up(u, k).start()
+                if s == 5 - k:
+                    @pl.when(z == k)
+                    def _():
+                        if k < 3:
+                            self.c_down(u, k + 1).wait_recv()
+                            self.add(u, self.part, 32 * k + 32, self.down_in.at[lax.rem(u, 4), pl.ds(0, 32 * k + 32)])
+                        if k > 0:
+                            self.c_down(u, k).start()
+        if s == 5:
+            self.c_last(u).start()
+        elif s == 6:
+            for k in range(4):
+                @pl.when(z == k)
+                def _():
+                    if k < 3:
+                        self.c_up(u, k).wait_send()
+                    if k > 0:
+                        self.c_down(u, k).wait_send()
+            self.c_last(u).wait()
+            self.add(u, self.part + 32 * z + 16 * self.far_bit, 16, self.last_in.at[u])
+            self.c_far(u).start()
+            self.c_own(u).start()
+        elif s == 7:
+            self.c_far(u).wait()
+            self.c_own(u).wait()
+        if 7 <= s <= 10:
+            hop = s - 7
+            if hop > 0:
+                @pl.when(z >= hop)
+                def _():
+                    self.c_rise_in(u, hop - 1).wait_recv()
+
+                @pl.when(z + hop < 4)
+                def _():
+                    self.c_fall_in(u, hop - 1).wait_recv()
+            if hop < 3:
+                @pl.when((z >= hop) & (z < 3))
+                def _():
+                    self.c_rise(u, hop).start()
+
+                @pl.when((z + hop < 4) & (z > 0))
+                def _():
+                    self.c_fall(u, hop).start()
+        if s == 10:
+            self.c_near(u).start()
+        elif s == 11:
+            for hop in range(3):
+                @pl.when((z >= hop) & (z < 3))
+                def _():
+                    self.c_rise(u, hop).wait_send()
+
+                @pl.when((z + hop < 4) & (z > 0))
+                def _():
+                    self.c_fall(u, hop).wait_send()
+            self.c_near(u).wait_send()
+            self.c_near_in(u).wait_recv()
+            self.c_sibling(u).start()
+        elif s == 12:
+            self.c_sibling(u).wait_send()
+            self.c_sibling_in(u).wait_recv()
+
+    def c_rise_in(self, u, hop):
+        piece = self.done(u, self.part + 32 * (self.z - 1 - hop), 32)
+        return self.copy(6 + hop, u, piece, piece, self.below)
+
+    def c_fall_in(self, u, hop):
+        piece = self.done(u, self.part + 32 * (self.z + 1 + hop), 32)
+        return self.copy(9 + hop, u, piece, piece, self.above)
+
+    def c_near_in(self, u):
+        piece = self.done(u, self.other_part, 128)
+        return self.copy(12, u, piece, piece, self.near)
+
+    def c_sibling_in(self, u):
+        piece = self.done(u, self.other_half, 256)
+        return self.copy(13, u, piece, piece, self.sibling)
+
+
+def scratch(units, slots, width):
+    f32 = jnp.float32
+    return [
+        pltpu.VMEM((slots, 512, width), f32),
+        pltpu.VMEM((2, 256, width), f32),
+        pltpu.VMEM((2, 128, width), f32),
+        pltpu.VMEM((4, 96, width), f32),
+        pltpu.VMEM((4, 96, width), f32),
+        pltpu.VMEM((units, 16, width), f32),
+        pltpu.SemaphoreType.DMA((KINDS, units)),
+        pltpu.SemaphoreType.DMA((KINDS, units)),
+        pltpu.SemaphoreType.DMA((units,)),
+    ]
+
+
+def sum_kernel(units, slots, packed, result, grads, half_in, part_in, up_in, down_in, last_in, send, recv, local, load):
+    ring = Summing(grads, slots, half_in, part_in, up_in, down_in, last_in, result, send, recv, local)
+    greet((ring.sibling, ring.near, ring.far))
+
+    def bring(u):
+        return pltpu.make_async_copy(packed.at[u], grads.at[lax.rem(u, slots)], load.at[lax.rem(u, 2)])
+
+    bring(0).start()
+
+    def tick(t, carry):
+        @pl.when(t < units)
+        def _():
+            bring(t).wait()
+
+        @pl.when(t + 1 < units)
+        def _():
+            bring(t + 1).start()
+        for s in reversed(range(STAGES)):
+            u = t - s
+
+            @pl.when((u >= 0) & (u < units))
+            def _():
+                ring.stage(s, u)
+        return carry
+
+    lax.fori_loop(0, units + STAGES - 1, tick, 0)
+
+
+def sum_all(packed, cid=0):
+    units, rows, width = packed.shape
+    slots = 10
+    return pl.pallas_call(
+        functools.partial(sum_kernel, units, slots),
+        out_shape=jax.ShapeDtypeStruct(packed.shape, jnp.float32),
+        in_specs=[pl.BlockSpec(memory_space=pl.ANY)],
+        out_specs=pl.BlockSpec(memory_space=pl.ANY),
+        scratch_shapes=scratch(units, slots, width) + [pltpu.SemaphoreType.DMA((2,))],
+        compiler_params=pltpu.CompilerParams(collective_id=cid, has_side_effects=True, vmem_limit_bytes=56 * 2**20),
+        name="sum_all",
+    )(packed)
 
 
 def carried_in(part, axis, combine, identity, reverse):
@@ -202,31 +470,20 @@
     )
     back_in_norm, grad_norm1 = norm1_pull(back_norm_one)
     back_inputs = (back_middle + back_in_norm).reshape(row_count, steps_dev, width)
-    (
-        grad_norm1,
-        grad_in,
-        grad_forget,
-        grad_input,
-        grad_out,
-        grad_norm2,
-        grad_up,
-        grad_up_bias,
-        grad_down,
-        grad_down_bias,
-    ) = lax.psum(
-        (
-            grad_norm1,
-            grad_in,
-            grad_forget,
-            grad_input,
-            grad_out,
-            grad_norm2,
-            grad_up,
-            grad_up_bias,
-            grad_down,
-            grad_down_bias,
-        ),
-        ("seq", "rows"),
+    if lax.axis_size("seq") == 8 and lax.axis_size("rows") == 4:
+        pieces = [grad_in[:, 512 * i : 512 * i + 512] for i in range(6)]
+        pieces += [grad_out[:512], grad_out[512:]]
+        pieces += [grad_up[:, 512 * i : 512 * i + 512] for i in range(4)]
+        pieces += [grad_down[512 * i : 512 * i + 512] for i in range(4)]
+        summed = sum_all(jnp.stack(pieces))
+        grad_in = jnp.concatenate([summed[i] for i in range(6)], axis=1)
+        grad_out = summed[6:8].reshape(1024, 512)
+        grad_up = jnp.concatenate([summed[8 + i] for i in range(4)], axis=1)
+        grad_down = summed[12:16].reshape(2048, 512)
+    else:
+        grad_in, grad_out, grad_up, grad_down = lax.psum((grad_in, grad_out, grad_up, grad_down), ("seq", "rows"))
+    grad_norm1, grad_forget, grad_input, grad_norm2, grad_up_bias, grad_down_bias = lax.psum(
+        (grad_norm1, grad_forget, grad_input, grad_norm2, grad_up_bias, grad_down_bias), ("seq", "rows")
     )
     return (
         mixed,

time: 925 us -> 877 us (0.948)
  waiting for transfers between devices: 206 us -> 0 us
  Pallas kernels: 0 us -> 159 us
  local copies, waits for them, and re-layouts: 99 us -> 126 us
  between operations: 14.7 us -> 1.65 us
  matrix products: 143 us -> 130 us
    psum x1 -> x0, waiting for transfers between devices: 206 us -> none  [on_device(): lax.psum((grad_norm1, grad_in, grad_forget, grad_input, grad_out, grad_no...]
    pallas_call x0 -> x1, Pallas kernels: none -> 159 us  [sum_all(): pl.pallas_call(functools.partial(sum_kernel, units, slots), out_shape=jax...]
    unnamed x89 -> x103, local copies, waits for them, and re-layouts: 18.2 us -> 32.7 us
  transfers between devices with their start and end apart: 1 -> 0, of which waited for: 1 -> 0; matrix products, arithmetic and copies ran while one was open for 3% -> 0% of each run, Pallas kernels for 0% -> 0%
where the time goes in v1:
time: 877 us; the launch traced here: 861 us
  other arithmetic  274 us (31%)
  blocking collectives  167 us (19%)
  Pallas kernels  159 us (18%)
  matrix products  130 us (15%)
  local copies, waits for them, and re-layouts  126 us (14%)
    pallas_call x1, Pallas kernels, sum_all(): pl.pallas_call(functools.partial(sum_kernel, units, slots), out_shape=jax...  159 us
    all_gather x4, blocking collectives, carried_in(): gathered = jax.tree.map(lambda a: lax.all_gather(a, axis), part)  127 us
    while x112, other arithmetic  107 us
    psum x1, blocking collectives, on_device(): lax.psum((grad_norm1, grad_forget, grad_input, grad_norm2, grad_up_bias,...  40.2 us
    dynamic_update_slice x48, local copies, waits for them, and re-layouts, on_device(): lax.scan(state_step, carried, (decay_blocks, update_blocks))  38.7 us
    dot_general x6, matrix products, right_dot(): lax.dot_general(left, right, (((1,), (1,)), ((), ())), preferred_element_...  37.1 us
    reduce_sum x1, other arithmetic, gate_terms(): log_input = -jax.nn.softplus(-(part_input + bias_input))  33.5 us
    unnamed x103, local copies, waits for them, and re-layouts  32.7 us

profile of v1, /device:TPU:0, one launch (start us, length us, event | category | flops | bytes accessed | tf_op | source)
XLA Modules:
  0.0 861.0 jit_solution(6908861549168924878)
XLA Ops:
  12.0 5.7 fusion.144
  23.4 24.7 %fusion.154 = (f32[2048,1024]{1,0:T(8,128)}, f32[2048,1024]{1,0:T(8,128)}, f32[2048,1024]{1,0:T(8,128)}) fusion(f32[2048,1024]{1,0:T(8,128)} %fusion.144, f32[1024]{0:T(1024)S(1)} %copy-done.30, f32[2048,1024]{1,0:T(8,128)} %fusion.147, f32[1024]{0:T(1024)S(1)} %copy-done.32, bf16[2048,512]{1,0:T(8,128)(2,1)S(1)} %fusion.108, ...), kind=kOutput, calls=%fused_computation.326 | convolution fusion | flops 2208301056 | bytes 45096960 | tf_op jit(solution)/shard_map/dot_general | solution.py:356
  48.1 11.7 %copy.42 = f32[128,16,1024]{2,1,0:T(8,128)} copy(f32[128,16,1024]{2,0,1:T(8,128)} %bitcast.788) | data formatting | bytes 16777216 | tf_op jit(solution)/shard_map/transpose | solution.py:361
  60.4 8.1 copy.41
  68.5 21.6 %while.90 = (s32[]{:T(128)}, f32[16,1024]{1,0:T(8,128)S(1)}, f32[16,1024]{1,0:T(8,128)S(1)}, f32[16,8,16,1024]{3,2,1,0:T(8,128)}, f32[16,8,16,1024]{3,2,1,0:T(8,...) while((s32[]{:T(128)}, f32[16,1024]{1,0:T(8,128)S(1)}, ...), condition=%wide.region_3.5_spmd.clone, body=%wide.region_2.4_spmd.clone.sunk | while | flops 425994 | bytes 1310987 | solution.py:375
  90.2 33.0 %all-gather.1 = f32[128,1024]{1,0:T(8,128)S(1)} all-gather(f32[16,1024]{1,0:T(8,128)S(1)} %get-tuple-element.415), channel_id=3, replica_groups=mesh['seq'=8,'rows'=4] {'seq'}, dimensions={0}, use_global_device_ids=true | all-gather | bytes 589824 | tf_op jit(solution)/shard_map/all_gather | solution.py:281
  123.2 31.3 %all-gather = f32[128,1024]{1,0:T(8,128)S(1)} all-gather(f32[16,1024]{1,0:T(8,128)S(1)} %get-tuple-element.414), channel_id=2, replica_groups=mesh['seq'=8,'rows'=4] {'seq'}, dimensions={0}, use_global_device_ids=true | all-gather | bytes 589824 | tf_op jit(solution)/shard_map/all_gather | solution.py:281
  158.7 140.8 %while.87 = (s32[]{:T(128)}, f32[16,1024]{1,0:T(8,128)S(1)}, bf16[16,8,16,1024]{3,2,1,0:T(8,128)(2,1)}, f32[16,8,16,1024]{3,2,1,0:T(8,128)}, f32[16,8,16,1024]{3...) while((s32[]{:T(128)}, f32[16,1024]{1,0:T(8,128)S(1)}, ...), condition=%wide.region_7.9_spmd, body=%wide.region_6.8_spmd.sunk | while | flops 262152 | bytes 4849965 | solution.py:392
  307.1 12.4 %multiply_convert_fusion = (bf16[2048,2048]{1,0:T(8,128)(2,1)}, f32[2048,2048]{1,0:T(8,128)}) fusion(f32[2048]{0:T(1024)S(1)} %copy-done.35, bf16[512,2048]{1,0:T(8,128)(2,1)S(1)} %copy-done, f32[2048,512]{1,0:T(8,128)S(1)} %get-tuple-element.584, f32[512]{0:T(512)S(1)} %copy-done.34, f32[2048]{0:T(1024)S(1)} %fusion.152), kind=kOutput, calls=%fused_computation.192 | convolution fusion | flops 4340056064 | bytes 31475712 | tf_op jit(solution)/shard_map/dot_general | solution.py:401
  319.5 18.8 %fusion.174 = (f32[2048]{0:T(1024)S(1)}, bf16[2048,2048]{1,0:T(8,128)(2,1)}) fusion(f32[2048,2048]{1,0:T(8,128)} %get-tuple-element.586, f32[2048]{0:T(1024)S(1)} %copy-done.35, bf16[2048,512]{1,0:T(8,128)(2,1)S(1)} %bitcast.786, bf16[2048,512]{1,0:T(8,128)(2,1)} %param.37), kind=kOutput, calls=%fused_computation.329 | convolution fusion | flops 4387239936 | bytes 29376512 | tf_op jit(solution)/shard_map/dot_general | solution.py:315
  338.3 10.1 %add_convert_fusion = bf16[2048,512]{1,0:T(8,128)(2,1)} fusion(f32[2048,512]{1,0:T(8,128)S(1)} %get-tuple-element.584, bf16[2048,2048]{1,0:T(8,128)(2,1)} %get-tuple-element.585, bf16[2048,512]{1,0:T(8,128)(2,1)} %param.37, f32[512]{0:T(512)S(1)} %copy-done.36), kind=kOutput, calls=%fused_computation.250 | convolution fusion | flops 4298113024 | bytes 16779264 | tf_op jit(solution)/shard_map/dot_general | solution.py:404
  348.4 6.1 fusion.176
  354.5 6.6 fusion.112
  361.1 5.8 multiply_reduce_fusion
  374.9 8.1 copy.44
  383.1 21.7 %while.91 = (s32[]{:T(128)}, f32[16,1024]{1,0:T(8,128)S(1)}, f32[16,1024]{1,0:T(8,128)S(1)}, f32[16,8,16,1024]{3,2,1,0:T(8,128)}, f32[16,8,16,1024]{3,2,1,0:T(8,...) while((s32[]{:T(128)}, f32[16,1024]{1,0:T(8,128)S(1)}, ...), condition=%wide.region_11.13_spmd.clone, body=%wide.region_10.12_spmd.clone.sunk | while | flops 425995 | bytes 1311007 | solution.py:429
  404.7 31.6 %all-gather.3 = f32[128,1024]{1,0:T(8,128)S(1)} all-gather(f32[16,1024]{1,0:T(8,128)S(1)} %get-tuple-element.419), channel_id=5, replica_groups=mesh['seq'=8,'rows'=4] {'seq'}, dimensions={0}, use_global_device_ids=true | all-gather | bytes 589824 | tf_op jit(solution)/shard_map/all_gather | solution.py:281
  436.3 31.4 %all-gather.2 = f32[128,1024]{1,0:T(8,128)S(1)} all-gather(f32[16,1024]{1,0:T(8,128)S(1)} %get-tuple-element.418), channel_id=4, replica_groups=mesh['seq'=8,'rows'=4] {'seq'}, dimensions={0}, use_global_device_ids=true | all-gather | bytes 589824 | tf_op jit(solution)/shard_map/all_gather | solution.py:281
  472.3 63.2 %while.89 = (s32[]{:T(128)}, f32[16,1024]{1,0:T(8,128)S(1)}, f32[16,8,16,1024]{3,2,1,0:T(8,128)}, f32[16,8,16,1024]{3,2,1,0:T(8,128)}, f32[16,8,16,1024]{3,2,1,0...) while((s32[]{:T(128)}, f32[16,1024]{1,0:T(8,128)S(1)}, ...), condition=%wide.region_15.17_spmd, body=%wide.region_14.16_spmd.sunk | while | flops 278537 | bytes 3801373 | solution.py:445
  535.5 17.4 %fusion.101 = (f32[128,16,1024]{2,0,1:T(8,128)S(1)}, f32[128,16,1024]{2,0,1:T(8,128)S(1)}) fusion(f32[128,16,1024]{2,1,0:T(8,128)} %bitcast.780, f32[128,16]{0,1:T(8,128)S(1)} %copy-done.25, f32[128,16,1024]{2,1,0:T(8,128)} %bitcast.781), kind=kLoop, calls=%fused_computation.215 | loop fusion | flops 4194304 | bytes 33562624 | tf_op jit(solution)/shard_map/mul | solution.py:449
  553.0 33.5 %fusion.170 = (f32[1024]{0:T(1024)S(1)}, f32[2048,1024]{1,0:T(8,128)}, f32[1024]{0:T(1024)S(1)}, f32[2048,1024]{1,0:T(8,128)}, bf16[2048,1024]{1,0:T(8,128)(2,1)}) fusion(f32[128,16,1024]{2,0,1:T(8,128)S(1)} %get-tuple-element.580, f32[2048,1024]{1,0:T(8,128)} %fusion.147, f32[1024]{0:T(1024)S(1)} %copy-done.33, f32[2048,1024]{1,0:T(8,128)} %fusion.144, ...), kind=kLoop, calls=%fused_computation.327 | loop fusion | flops 134215680 | bytes 62930944 | tf_op jit(solution)/shard_map/transpose(jvp())/reduce_sum | solution.py:299
  586.6 7.3 fusion.118
  615.1 40.2 %all-reduce = (f32[512]{0:T(512)}, f32[1024]{0:T(1024)}, f32[1024]{0:T(1024)}, f32[512]{0:T(512)}, f32[2048]{0:T(1024)}, /*index=5*/f32[512]{0:T(512)}) all-reduce(f32[512]{0:T(512)S(1)} %get-tuple-element.463, f32[1024]{0:T(1024)S(1)} %neg.51, f32[1024]{0:T(1024)S(1)} %neg.52, ...), channel_id=1, replica_groups=mesh['seq'=8,'rows'=4] {'seq','rows'}, use_global_device_ids=true, to_apply=%region_18.20 | all-reduce | flops 5632 | bytes 45056 | tf_op jit(solution)/shard_map/psum | solution.py:485
  677.8 159.4 %sum_all.1 = f32[16,512,512]{2,1,0:T(8,128)} custom-call(f32[16,512,512]{2,1,0:T(8,128)} %fusion.120.packed), custom_call_target="tpu_custom_call" | custom-call | tf_op jit(solution)/shard_map/sum_all/pallas_call | solution.py:266
  (537 shorter events, 353.9 us)
Async XLA Ops:
  0.6 306.4 %copy-start = (bf16[512,2048]{1,0:T(8,128)(2,1)S(1)}, bf16[512,2048]{1,0:T(8,128)(2,1)}, u32[]{:S(2)}) copy-start(bf16[512,2048]{1,0:T(8,128)(2,1)} %param.35) | copy-start | bytes 6291460
  6.0 11.7 %copy-start.21 = (f32[2048]{0:T(1024)}, f32[2048]{0:T(1024)S(1)}, u32[]{:S(2)}) copy-start(f32[2048]{0:T(1024)S(1)} %bitcast_rsqrt_fusion) | copy-start | bytes 24580
  6.9 52.9 %copy-start.24 = (f32[128,16]{0,1:T(8,128)}, f32[128,16]{0,1:T(8,128)S(1)}, u32[]{:S(2)}) copy-start(f32[128,16]{0,1:T(8,128)S(1)} %select_bitcast_fusion) | copy-start | bytes 24580
  9.2 14.2 %copy-start.16 = (bf16[2048,512]{1,0:T(8,128)(2,1)}, bf16[2048,512]{1,0:T(8,128)(2,1)S(1)}, u32[]{:S(2)}) copy-start(bf16[2048,512]{1,0:T(8,128)(2,1)S(1)} %fusion.108) | copy-start | bytes 6291460
  48.1 11.7 %copy-start.9 = (f32[2048,1024]{1,0:T(8,128)S(1)}, f32[2048,1024]{1,0:T(8,128)}, u32[]{:S(2)}) copy-start(f32[2048,1024]{1,0:T(8,128)} %get-tuple-element.575) | copy-start | bytes 25165828
  307.1 12.4 %copy-start.8 = (bf16[16,128,512]{2,1,0:T(8,128)(2,1)S(1)}, bf16[16,128,512]{2,1,0:T(8,128)(2,1)}, u32[]{:S(2)}) copy-start(bf16[16,128,512]{2,1,0:T(8,128)(2,1)} %param.27) | copy-start | bytes 6291460
  319.5 18.8 %copy-start.36 = (f32[512]{0:T(512)S(1)}, f32[512]{0:T(512)}, u32[]{:S(2)}) copy-start(f32[512]{0:T(512)} %param.38) | copy-start | bytes 6148
  338.3 10.2 %copy-start.38 = (bf16[2048,2048]{1,0:T(8,128)(2,1)S(1)}, bf16[2048,2048]{1,0:T(8,128)(2,1)}, u32[]{:S(2)}) copy-start(bf16[2048,2048]{1,0:T(8,128)(2,1)} %get-tuple-element.585) | copy-start | bytes 25165828
  348.4 6.1 copy-start.37
  368.7 6.2 copy-start.2
  374.9 8.2 copy-start.12
  374.9 8.1 copy-start.13
  472.3 63.2 %copy-start.25 = (f32[128,16]{0,1:T(8,128)S(1)}, f32[128,16]{0,1:T(8,128)}, u32[]{:S(2)}) copy-start(f32[128,16]{0,1:T(8,128)} %copy-done.24) | copy-start | bytes 24580
  535.5 17.5 %copy-start.31 = (f32[1024]{0:T(1024)S(1)}, f32[1024]{0:T(1024)}, u32[]{:S(2)}) copy-start(f32[1024]{0:T(1024)} %param.32) | copy-start | bytes 12292
  535.5 17.5 %copy-start.33 = (f32[1024]{0:T(1024)S(1)}, f32[1024]{0:T(1024)}, u32[]{:S(2)}) copy-start(f32[1024]{0:T(1024)} %param.31) | copy-start | bytes 12292
  553.0 33.6 %copy-start.17 = (bf16[2048,512]{1,0:T(8,128)(2,1)S(1)}, bf16[2048,512]{1,0:T(8,128)(2,1)}, u32[]{:S(2)}) copy-start(bf16[2048,512]{1,0:T(8,128)(2,1)} %copy-done.16) | copy-start | bytes 6291460
  586.6 7.4 copy-start.7
  586.6 7.4 copy-start.20
  586.6 9.9 %slice-start = ((s8[8388608]{0:T(1024)(128)(4,1)}), s8[4194304]{0:T(1024)(128)(4,1)S(1)}, s32[]{:S(2)}) async-start(s8[8388608]{0:T(1024)(128)(4,1)} %bitcast.784), calls=%async_computation | async-start | bytes 8388608
  615.1 51.9 %copy-start.14 = (f32[1024,512]{1,0:T(8,128)S(1)}, f32[1024,512]{1,0:T(8,128)}, u32[]{:S(2)}) copy-start(f32[1024,512]{1,0:T(8,128)} %fusion.136) | copy-start | bytes 6291460
  655.3 9.4 %copy-start.15 = (f32[512,1024]{1,0:T(8,128)S(1)}, f32[512,1024]{1,0:T(8,128)}, u32[]{:S(2)}) copy-start(f32[512,1024]{1,0:T(8,128)} %fusion.175) | copy-start | bytes 6291460
  655.3 13.8 %copy-start.11 = (f32[512,2048]{1,0:T(8,128)S(1)}, f32[512,2048]{1,0:T(8,128)}, u32[]{:S(2)}) copy-start(f32[512,2048]{1,0:T(8,128)} %fusion.112) | copy-start | bytes 12582916
  664.8 8.8 %copy-start.10 = (f32[2048,512]{1,0:T(8,128)S(1)}, f32[2048,512]{1,0:T(8,128)}, u32[]{:S(2)}) copy-start(f32[2048,512]{1,0:T(8,128)} %fusion.176) | copy-start | bytes 12582916
  847.5 13.0 %copy-start.1 = (bf16[512,2048]{1,0:T(8,128)(2,1)S(1)}, bf16[512,2048]{1,0:T(8,128)(2,1)}, u32[]{:S(2)}) copy-start(bf16[512,2048]{1,0:T(8,128)(2,1)} %param.35) | copy-start | bytes 6291460
  (17 other events, 58.8 us)

commit v2 on v1

v2 whole, which is shorter than its diff:
```python
import functools
import math
import jax
import jax.numpy as jnp
from jax import lax
from jax.experimental import pallas as pl
from jax.experimental.pallas import tpu as pltpu
from jax.sharding import PartitionSpec as P

MESH = pl.DeviceIdType.MESH
EPS = 1e-6
F32 = jnp.float32
BF16 = jnp.bfloat16
STAGES = 13
KINDS = 14


def place():
    seq = lax.axis_index("seq")
    rows = lax.axis_index("rows")
    return lax.div(rows, 2), lax.rem(seq, 2), lax.div(seq, 2), lax.rem(rows, 2)


def spot(x, y, z, core):
    return (z * 2 + y, x * 2 + core)


def dot(left, right):
    return jnp.dot(left, right, preferred_element_type=F32)


def dot_nt(left, right):
    return lax.dot_general(left, right, (((1,), (1,)), ((), ())), preferred_element_type=F32)


def dot_tn(left, right):
    return lax.dot_general(left, right, (((0,), (0,)), ((), ())), preferred_element_type=F32)


class Chain:
    def __init__(self, count, sign, sent, got, join, send, recv):
        self.count, self.sign = count, sign
        self.sent, self.got, self.join = sent, got, join
        self.send, self.recv = send, recv
        self.rounds = max(1, math.ceil(math.log2(count)))
        seq = lax.axis_index("seq")
        self.seq = seq
        self.place = seq if sign > 0 else count - 1 - seq

    def partners(self):
        for r in range(self.rounds):
            far = 2**r
            yield self.seq + self.sign * far, self.place + far < self.count
            yield self.seq - self.sign * far, self.place >= far

    def copy(self, part, r, other):
        return pltpu.make_async_remote_copy(
            src_ref=self.sent.at[part, r], dst_ref=self.got.at[part, r],
            send_sem=self.send.at[part, r], recv_sem=self.recv.at[part, r],
            device_id=(other, lax.axis_index("rows")), device_id_type=MESH,
        )

    def push(self, part, r):
        @pl.when(self.place + 2**r < self.count)
        def _():
            self.copy(part, r, self.seq + self.sign * 2**r).start()

    def start(self, part, product, end):
        self.sent[part, 0, 0] = product
        self.sent[part, 0, 1] = end
        self.join[part, 0] = jnp.ones_like(product)
        self.join[part, 1] = jnp.zeros_like(end)
        self.push(part, 0)

    def advance(self, part, r):
        last = r == self.rounds - 1

        @pl.when(self.place >= 2**r)
        def _():
            self.copy(part, r, self.seq - self.sign * 2**r).wait_recv()
            product, end = self.got[part, r, 0], self.got[part, r, 1]
            own = self.join[part, 0]
            self.join[part, 1] = self.join[part, 1] + own * end
            if not last:
                self.join[part, 0] = own * product
                here = self.sent[part, r, 0]
                self.sent[part, r + 1, 0] = here * product
                self.sent[part, r + 1, 1] = self.sent[part, r, 1] + here * end

        if not last:
            @pl.when(self.place < 2**r)
            def _():
                self.sent[part, r + 1] = self.sent[part, r]
            self.push(part, r + 1)

    def finish(self, part):
        for r in range(self.rounds):
            @pl.when(self.place + 2**r < self.count)
            def _():
                self.copy(part, r, self.seq + self.sign * 2**r).wait_send()


def greet_chain(chain):
    barrier = pltpu.get_barrier_semaphore()
    rows = lax.axis_index("rows")
    total = 0
    for other, there in chain.partners():
        @pl.when(there)
        def _():
            pl.semaphore_signal(barrier, inc=1, device_id=(other, rows), device_id_type=MESH)
        total = total + jnp.where(there, 1, 0)
    return barrier, total


def chain_scratch(parts, count, rows, width):
    rounds = max(1, math.ceil(math.log2(count)))
    return [
        pltpu.VMEM((parts, rounds, 2, rows, width), F32),
        pltpu.VMEM((parts, rounds, 2, rows, width), F32),
        pltpu.VMEM((parts, 2, rows, width), F32),
        pltpu.SemaphoreType.DMA((parts, rounds)),
        pltpu.SemaphoreType.DMA((parts, rounds)),
    ]


def front_kernel(
    count, rows, steps, chunk, block,
    tokens, cotangent, reset, gain, w_in, forget_bias, input_bias, w_out,
    x_out, cot_out, middle_out, state_out, decay_out, fade_out, rise_out, weight_out, lean_out,
    tok_v, cot_v, x_v, normed_v, w_v, w_out_v, keep_v, decay_v, update_v, cand_v, fade_v, rise_v, weight_v, lean_v, state_v, middle_v,
    sent, got, join, send, recv, sems, out_sems,
):
    total, width = x_v.shape
    hidden = w_out_v.shape[0]
    parts = hidden // chunk
    size = block * rows
    blocks = steps // block
    chain = Chain(count, 1, sent, got, join, send, recv)
    barrier, greeted = greet_chain(chain)
    loads = [pltpu.make_async_copy(tokens, tok_v, sems.at[0])]
    for j in range(parts):
        for k in range(3):
            loads.append(pltpu.make_async_copy(w_in.at[:, pl.ds(k * hidden + j * chunk, chunk)], w_v.at[j, :, pl.ds(k * chunk, chunk)], sems.at[1 + 3 * j + k]))
    loads.append(pltpu.make_async_copy(cotangent, cot_v, sems.at[1 + 3 * parts]))
    loads.append(pltpu.make_async_copy(w_out, w_out_v, sems.at[2 + 3 * parts]))
    for load in loads:
        load.start()
    loads[0].wait()

    first = lax.axis_index("seq") * steps
    marks = [jnp.broadcast_to(reset[:, k : k + 1], (rows, 128)) for k in range(reset.shape[1])]

    def mark(t, carry):
        hit = marks[0] == first + t
        for one in marks[1:]:
            hit = hit | (one == first + t)
        keep_v[pl.ds(pl.multiple_of(t * rows, rows), rows)] = jnp.where(hit, 0.0, 1.0)
        return carry

    lax.fori_loop(0, steps, mark, 0, unroll=4)
    gains = gain[...]

    def norm(b, carry):
        at = pl.ds(pl.multiple_of(b * size, size), size)
        x = tok_v[:, pl.ds(pl.multiple_of(b * block, block), block), :].astype(F32)
        x = jnp.swapaxes(x, 0, 1).reshape(size, width)
        x_v[at] = x.astype(BF16)
        scale = lax.rsqrt(jnp.mean(x * x, axis=-1, keepdims=True) + EPS)
        normed_v[at] = (x * scale * gains).astype(BF16)
        return carry

    lax.fori_loop(0, blocks, norm, 0)
    outs = [pltpu.make_async_copy(x_v, x_out, out_sems.at[0])]
    outs[0].start()

    def gates(j):
        lanes = pl.ds(j * chunk, chunk)
        shift_f, shift_i = -forget_bias[:, lanes], -input_bias[:, lanes]

        def one(b, carry):
            product, end = carry
            at = pl.ds(pl.multiple_of(b * size, size), size)
            project = dot(normed_v[at], w_v[j])
            neg_f = shift_f - project[:, :chunk]
            neg_i = shift_i - project[:, chunk : 2 * chunk]
            cand = project[:, 2 * chunk :]
            lower = jnp.maximum(jnp.minimum(neg_f, neg_i) - 20.0, 0.0)
            exp_f = jnp.exp(jnp.minimum(neg_f - lower, 80.0))
            exp_i = jnp.exp(jnp.minimum(neg_i - lower, 80.0))
            one_f, one_i = 1.0 + exp_f, 1.0 + exp_i
            share = 1.0 / (one_f + one_i)
            decay, weight = one_i * share, one_f * share
            fade_v[j % 2, at] = (decay * (exp_f * share)).astype(BF16)
            rise_v[j % 2, at] = (weight * (exp_i * share)).astype(BF16)
            weight_v[j % 2, at] = weight.astype(BF16)
            cand_v[at, lanes] = cand
            update = weight * cand
            update_v[at, lanes] = update
            keep = jnp.concatenate([keep_v[at]] * (chunk // 128), axis=1)
            decay = decay * keep
            decay_v[at, lanes] = decay
            for t in range(block):
                here = decay[t * rows : (t + 1) * rows]
                end = here * end + update[t * rows : (t + 1) * rows]
                product = here * product
            return product, end

        start = (jnp.ones((rows, chunk), F32), jnp.zeros((rows, chunk), F32))
        return lax.fori_loop(0, blocks, one, start)

    def scan(j):
        lanes = pl.ds(j * chunk, chunk)

        def one(b, state):
            at = pl.ds(pl.multiple_of(b * size, size), size)
            states = []
            for t in range(block):
                here = pl.ds(pl.multiple_of(b * size + t * rows, rows), rows)
                keep = jnp.concatenate([keep_v[here]] * (chunk // 128), axis=1)
                lean_v[j % 2, here] = (keep * state - cand_v[here, lanes]).astype(BF16)
                state = decay_v[here, lanes] * state + update_v[here, lanes]
                states.append(state.astype(BF16))
            low = jnp.concatenate(states, axis=0)
            state_v[at, lanes] = low
            add = dot(low, w_out_v[lanes])
            if j == 0:
                middle_v[at] = x_v[at].astype(F32) + add
            else:
                middle_v[at] = middle_v[at] + add
            return state

        lax.fori_loop(0, blocks, one, join[j, 1])

    def put(source, target, slot, wait=False):
        copy = pltpu.make_async_copy(source, target, out_sems.at[slot])
        if wait:
            copy.wait()
        else:
            copy.start()

    def gate_outs(j, wait=False):
        lanes = pl.ds(j * chunk, chunk)
        for k, (a, b) in enumerate(((fade_v, fade_out), (rise_v, rise_out), (weight_v, weight_out))):
            put(a.at[j % 2], b.at[:, lanes], 1 + 3 * j + k, wait)
        put(decay_v.at[:, lanes], decay_out.at[:, lanes], 1 + 3 * parts + j, wait)

    def scan_outs(j, wait=False):
        lanes = pl.ds(j * chunk, chunk)
        put(lean_v.at[j % 2], lean_out.at[:, lanes], 1 + 4 * parts + 2 * j, wait)
        put(state_v.at[:, lanes], state_out.at[:, lanes], 2 + 4 * parts + 2 * j, wait)

    ready = 0
    for j in range(parts):
        for k in range(3):
            loads[1 + 3 * j + k].wait()
        if j >= 2:
            gate_outs(j - 2, True)
        product, end = gates(j)
        gate_outs(j)
        if j == 0:
            pl.semaphore_wait(barrier, greeted)
        chain.start(j, product, end)
        for i in range(j - 1, -1, -1):
            if j - 1 - i < chain.rounds:
                chain.advance(i, j - 1 - i)
    for k in range(2):
        loads[1 + 3 * parts + k].wait()

    def turn(b, carry):
        at = pl.ds(pl.multiple_of(b * size, size), size)
        c = cot_v[:, pl.ds(pl.multiple_of(b * block, block), block), :].astype(F32)
        normed_v[at] = jnp.swapaxes(c, 0, 1).reshape(size, width).astype(BF16)
        return carry

    lax.fori_loop(0, blocks, turn, 0)
    put(normed_v, cot_out, 1 + 6 * parts)

    step = parts - 1
    while ready < parts:
        for i in range(parts - 1, -1, -1):
            if 0 <= step - 1 - i < chain.rounds and step >= parts:
                chain.advance(i, step - 1 - i)
        while ready < parts and ready + chain.rounds <= step:
            if ready >= 2:
                scan_outs(ready - 2, True)
            scan(ready)
            scan_outs(ready)
            ready += 1
        step += 1
    put(middle_v, middle_out, 2 + 6 * parts)
    for j in range(parts):
        if j >= parts - 2:
            gate_outs(j, True)
            scan_outs(j, True)
        chain.finish(j)
    outs[0].wait()
    put(normed_v, cot_out, 1 + 6 * parts, True)
    put(middle_v, middle_out, 2 + 6 * parts, True)


def front(tokens, cotangent, reset, gain, w_in, forget_bias, input_bias, w_out, cid=1):
    rows, steps, width = tokens.shape
    hidden = w_out.shape[0]
    total = rows * steps
    count = lax.axis_size("seq")
    chunk, block = 256, 16
    parts = hidden // chunk
    anywhere = pl.BlockSpec(memory_space=pl.ANY)
    vmem = pl.BlockSpec(memory_space=pltpu.VMEM)
    shape = jax.ShapeDtypeStruct
    return pl.pallas_call(
        functools.partial(front_kernel, count, rows, steps, chunk, block),
        out_shape=(
            shape((total, width), BF16), shape((total, width), BF16), shape((total, width), F32),
            shape((total, hidden), BF16), shape((total, hidden), F32), shape((total, hidden), BF16),
            shape((total, hidden), BF16), shape((total, hidden), BF16), shape((total, hidden), BF16),
        ),
        in_specs=[anywhere, anywhere, vmem, vmem, anywhere, vmem, vmem, anywhere],
        out_specs=(anywhere,) * 9,
        scratch_shapes=[
            pltpu.VMEM(tokens.shape, BF16), pltpu.VMEM(tokens.shape, BF16), pltpu.VMEM((total, width), BF16), pltpu.VMEM((total, width), BF16),
            pltpu.VMEM((parts, width, 3 * chunk), BF16), pltpu.VMEM(w_out.shape, BF16), pltpu.VMEM((total, 128), F32),
            pltpu.VMEM((total, hidden), F32), pltpu.VMEM((total, hidden), F32), pltpu.VMEM((total, hidden), F32),
            pltpu.VMEM((2, total, chunk), BF16), pltpu.VMEM((2, total, chunk), BF16), pltpu.VMEM((2, total, chunk), BF16),
            pltpu.VMEM((2, total, chunk), BF16), pltpu.VMEM((total, hidden), BF16), pltpu.VMEM((total, width), F32),
            *chain_scratch(parts, count, rows, chunk),
            pltpu.SemaphoreType.DMA((3 + 3 * parts,)), pltpu.SemaphoreType.DMA((3 + 6 * parts,)),
        ],
        compiler_params=pltpu.CompilerParams(collective_id=cid, has_side_effects=True, vmem_limit_bytes=62 * 2**20),
        cost_estimate=pl.CostEstimate(flops=2 * total * width * 4 * hidden, bytes_accessed=40 * 2**20, transcendentals=3 * total * hidden),
        name="front",
    )(tokens, cotangent, reset, gain.reshape(1, -1), w_in, forget_bias.reshape(1, -1), input_bias.reshape(1, -1), w_out)


class Summing:
    def __init__(self, span, grads, slots, half_in, part_in, up_in, down_in, last_in, result, send, recv, local):
        self.grads, self.slots = grads, slots
        self.half_in, self.part_in, self.up_in, self.down_in, self.last_in = half_in, part_in, up_in, down_in, last_in
        self.result, self.send, self.recv, self.local = result, send, recv, local
        x, y, z, core = place()
        self.z = z
        first = core == 0
        self.sibling = spot(x, y, z, 1 - core)
        along_x, along_y = spot(1 - x, y, z, core), spot(x, 1 - y, z, core)
        self.near = tuple(jnp.where(first, a, b) for a, b in zip(along_x, along_y))
        self.far = tuple(jnp.where(first, b, a) for a, b in zip(along_x, along_y))
        self.above = spot(x, y, z + 1, core)
        self.below = spot(x, y, z - 1, core)
        near_bit = jnp.where(first, x, y)
        far_bit = jnp.where(first, y, x)
        self.n_half, self.n_part, self.n_line, self.n_tip = span // 2, span // 4, span // 16, span // 32
        self.half = core * self.n_half
        self.other_half = (1 - core) * self.n_half
        self.part = self.half + near_bit * self.n_part
        self.other_part = self.half + (1 - near_bit) * self.n_part
        self.tip = self.part + self.n_line * z + self.n_tip * far_bit
        self.other_tip = self.part + self.n_line * z + self.n_tip * (1 - far_bit)

    def copy(self, kind, unit, source, target, device):
        return pltpu.make_async_remote_copy(
            src_ref=source, dst_ref=target, send_sem=self.send.at[kind, unit], recv_sem=self.recv.at[kind, unit],
            device_id=device, device_id_type=MESH,
        )

    def rows(self, unit, start, count):
        return self.grads.at[lax.rem(unit, self.slots), pl.ds(pl.multiple_of(start, 8), count)]

    def done(self, unit, start, count):
        return self.result.at[unit, pl.ds(pl.multiple_of(start, 8), count)]

    def c_half(self, u):
        return self.copy(0, u, self.rows(u, self.other_half, self.n_half), self.half_in.at[lax.rem(u, 2)], self.sibling)

    def c_part(self, u):
        return self.copy(1, u, self.rows(u, self.other_part, self.n_part), self.part_in.at[lax.rem(u, 2)], self.near)

    def c_up(self, u, z):
        low, rest = self.n_line * (z + 1), self.n_line * (3 - z)
        return self.copy(2, u, self.rows(u, self.part + low, rest), self.up_in.at[lax.rem(u, 4), pl.ds(low - self.n_line, rest)], self.above)

    def c_down(self, u, z):
        rest = self.n_line * z
        return self.copy(3, u, self.rows(u, self.part, rest), self.down_in.at[lax.rem(u, 4), pl.ds(0, rest)], self.below)

    def c_last(self, u):
        return self.copy(4, u, self.rows(u, self.other_tip, self.n_tip), self.last_in.at[u], self.far)

    def c_own(self, u):
        return pltpu.make_async_copy(self.rows(u, self.tip, self.n_tip), self.done(u, self.tip, self.n_tip), self.local.at[u])

    def c_far(self, u):
        return self.copy(5, u, self.rows(u, self.tip, self.n_tip), self.done(u, self.tip, self.n_tip), self.far)

    def c_rise(self, u, hop, back=0):
        piece = self.done(u, self.part + self.n_line * (self.z - hop - back), self.n_line)
        return self.copy(6 + hop, u, piece, piece, self.above)

    def c_fall(self, u, hop, back=0):
        piece = self.done(u, self.part + self.n_line * (self.z + hop + back), self.n_line)
        return self.copy(9 + hop, u, piece, piece, self.below)

    def c_near(self, u, start):
        piece = self.done(u, start, self.n_part)
        return self.copy(12, u, piece, piece, self.near)

    def c_sibling(self, u, start):
        piece = self.done(u, start, self.n_half)
        return self.copy(13, u, piece, piece, self.sibling)

    def add(self, u, start, count, ref):
        slot = lax.rem(u, self.slots)
        step = math.gcd(count, 32)

        def one(i, carry):
            here = pl.ds(pl.multiple_of(start + i * step, 8), step)
            there = pl.ds(pl.multiple_of(i * step, 8), step)
            self.grads[slot, here] = self.grads[slot, here] + ref[there]
            return carry

        if count == step:
            one(0, 0)
        else:
            lax.fori_loop(0, count // step, one, 0)

    def stage(self, s, u):
        z = self.z
        if s == 0:
            self.c_half(u).start()
        elif s == 1:
            self.c_half(u).wait()
            self.add(u, self.half, self.n_half, self.half_in.at[lax.rem(u, 2)])
            self.c_part(u).start()
        elif s == 2:
            self.c_part(u).wait()
            self.add(u, self.part, self.n_part, self.part_in.at[lax.rem(u, 2)])
        if 2 <= s <= 5:
            for k in range(4):
                if s == 2 + k:
                    @pl.when(z == k)
                    def _():
                        if k > 0:
                            self.c_up(u, k - 1).wait_recv()
                            low, rest = self.n_line * k, self.n_line * (4 - k)
                            self.add(u, self.part + low, rest, self.up_in.at[lax.rem(u, 4), pl.ds(low - self.n_line, rest)])
                        if k < 3:
                            self.c_up(u, k).start()
                if s == 5 - k:
                    @pl.when(z == k)
                    def _():
                        if k < 3:
                            self.c_down(u, k + 1).wait_recv()
                            rest = self.n_line * (k + 1)
                            self.add(u, self.part, rest, self.down_in.at[lax.rem(u, 4), pl.ds(0, rest)])
                        if k > 0:
                            self.c_down(u, k).start()
        if s == 5:
            self.c_last(u).start()
        elif s == 6:
            for k in range(4):
                @pl.when(z == k)
                def _():
                    if k < 3:
                        self.c_up(u, k).wait_send()
                    if k > 0:
                        self.c_down(u, k).wait_send()
            self.c_last(u).wait()
            self.add(u, self.tip, self.n_tip, self.last_in.at[u])
            self.c_far(u).start()
            self.c_own(u).start()
        elif s == 7:
            self.c_far(u).wait()
            self.c_own(u).wait()
        if 7 <= s <= 10:
            hop = s - 7
            if hop > 0:
                @pl.when(z >= hop)
                def _():
                    self.c_rise(u, hop - 1, 1).wait_recv()

                @pl.when(z + hop < 4)
                def _():
                    self.c_fall(u, hop - 1, 1).wait_recv()
            if hop < 3:
                @pl.when((z >= hop) & (z < 3))
                def _():
                    self.c_rise(u, hop).start()

                @pl.when((z + hop < 4) & (z > 0))
                def _():
                    self.c_fall(u, hop).start()
        if s == 10:
            self.c_near(u, self.part).start()
        elif s == 11:
            for hop in range(3):
                @pl.when((z >= hop) & (z < 3))
                def _():
                    self.c_rise(u, hop).wait_send()

                @pl.when((z + hop < 4) & (z > 0))
                def _():
                    self.c_fall(u, hop).wait_send()
            self.c_near(u, self.part).wait_send()
            self.c_near(u, self.other_part).wait_recv()
            self.c_sibling(u, self.half).start()
        elif s == 12:
            self.c_sibling(u, self.half).wait_send()
            self.c_sibling(u, self.other_half).wait_recv()


def sum_scratch(units, slots, span, width):
    return [
        pltpu.VMEM((slots, span, width), F32),
        pltpu.VMEM((2, span // 2, width), F32),
        pltpu.VMEM((2, span // 4, width), F32),
        pltpu.VMEM((4, 3 * span // 16, width), F32),
        pltpu.VMEM((4, 3 * span // 16, width), F32),
        pltpu.VMEM((units, span // 32, width), F32),
        pltpu.SemaphoreType.DMA((KINDS, units)),
        pltpu.SemaphoreType.DMA((KINDS, units)),
        pltpu.SemaphoreType.DMA((units,)),
    ]


def greet_ring(ring):
    barrier = pltpu.get_barrier_semaphore()
    for there in (ring.sibling, ring.near, ring.far):
        pl.semaphore_signal(barrier, inc=1, device_id=there, device_id_type=MESH)

    @pl.when(ring.z > 0)
    def _():
        pl.semaphore_signal(barrier, inc=1, device_id=ring.below, device_id_type=MESH)

    @pl.when(ring.z < 3)
    def _():
        pl.semaphore_signal(barrier, inc=1, device_id=ring.above, device_id_type=MESH)

    return 3 + jnp.where(ring.z > 0, 1, 0) + jnp.where(ring.z < 3, 1, 0)


GELU_A = math.sqrt(2.0 / math.pi)
GELU_B = GELU_A * 0.044715
UNIT = 512
SMALL_ROWS = 256


def back_kernel(
    ringed, count, rows, steps, units, slots, holes, block,
    x_in, cot_in, middle_in, state_in, decay_in, fade_in, rise_in, weight_in, lean_in,
    gain_one, gain_two, up_bias, down_bias, w_in, w_out, w_up, w_down,
    mixed_out, tokens_out, result, small_out,
    middle_v, second_v, mixed_v, flow_v, state_v, cot_v, x_v, low_v, turned_v, w_in_v, w_out_v, w_up_v, w_down_v,
    decay_s, fade_s, rise_s, weight_s, lean_s, mixed_s, tokens_s, sums_v,
    load_sems, stream_sems, stage_sems,
    sent, got, join, send, recv,
    *ring_refs,
):
    total, width = x_v.shape
    hidden = w_out_v.shape[0]
    inner = w_down_v.shape[0]
    size = block * rows
    blocks = steps // block
    wide = UNIT
    halves = hidden // wide
    big = 512
    chain = Chain(count, -1, sent, got, join, send, recv)
    barrier, greeted = greet_chain(chain)
    grads = ring_refs[0]
    if ringed:
        ring = Summing(UNIT, grads, slots, *ring_refs[1:6], result, *ring_refs[6:9])
        small = Summing(SMALL_ROWS, ring_refs[9], 1, *ring_refs[10:15], small_out, *ring_refs[15:18])
        greeted = greeted + greet_ring(ring)
        small_v = ring_refs[9].at[0]
    else:
        small_v = ring_refs[1].at[0]

    loads = [
        pltpu.make_async_copy(source, target, load_sems.at[k])
        for k, (source, target) in enumerate((
            (middle_in, middle_v), (w_up, w_up_v), (cot_in, cot_v), (w_down, w_down_v), (state_in, state_v),
            (w_out, w_out_v), (w_in, w_in_v), (x_in, x_v),
        ))
    ]
    for load in loads:
        load.start()

    def at_block(b, n=size):
        return pl.ds(pl.multiple_of(b * n, n), n)

    def stage_at(t, s):
        v = t - s
        if isinstance(v, int):
            u = v - sum(hole < v for hole in holes)
            if 0 <= v and v not in holes and u <= units:
                ring.stage(s, u) if u < units else small.stage(s, 0)
            return
        u, real = v, v >= 0
        for hole in holes:
            u = u - jnp.where(v > hole, 1, 0)
            real = real & (v != hole)

        @pl.when(real & (u < units))
        def _():
            ring.stage(s, u)

        @pl.when(real & (u == units))
        def _():
            small.stage(s, 0)

    def tick(t):
        if ringed:
            for s in reversed(range(STAGES)):
                stage_at(t, s)

    def put_units(first, number):
        if not ringed:
            for k in range(number):
                copy = pltpu.make_async_copy(grads.at[lax.rem(first + k, slots)], result.at[first + k], load_sems.at[0])
                copy.start()
                copy.wait()

    sums_v[...] = jnp.zeros_like(sums_v)
    small_v[...] = jnp.zeros_like(small_v)

    def put_small(row, value):
        for k in range(value.shape[1] // 128):
            small_v[pl.ds(row + k, 1)] = value[:, 128 * k : 128 * k + 128]

    loads[0].wait()
    gains = gain_two[...]
    bias = down_bias[...]

    def norm_two(b, carry):
        at = at_block(b)
        value = middle_v[at]
        scale = lax.rsqrt(jnp.mean(value * value, axis=-1, keepdims=True) + EPS)
        normed = value * scale * gains
        low_v[at] = normed.astype(BF16)
        turned_v[:, at] = jnp.swapaxes(normed, 0, 1).astype(BF16)
        mixed_v[at] = value + bias
        second_v[at] = jnp.zeros_like(value)
        return carry

    lax.fori_loop(0, blocks, norm_two, 0)
    for k in (1, 2, 3):
        loads[k].wait()
    pl.semaphore_wait(barrier, greeted)

    def feed(f, tok):
        at = at_block(tok, big)
        lanes = pl.ds(pl.multiple_of(f * UNIT, UNIT), UNIT)
        cot = cot_v[at]
        pre = dot(low_v[at], w_up_v[:, lanes]) + up_bias[:, lanes]
        back_act = dot_nt(cot, w_down_v[lanes])
        square = pre * pre
        gate = 0.5 * jnp.tanh(pre * (GELU_A + GELU_B * square)) + 0.5
        act = pre * gate
        slope = gate + act * (1.0 - gate) * (2.0 * GELU_A + 6.0 * GELU_B * square)
        back_up = back_act * slope
        sums_v[0:1, lanes] = sums_v[0:1, lanes] + jnp.sum(back_up, axis=0, keepdims=True)
        act, back_up = act.astype(BF16), back_up.astype(BF16)
        mixed_v[at] = mixed_v[at] + dot(act, w_down_v[lanes])
        second_v[at] = second_v[at] + dot_nt(back_up, w_up_v[:, lanes])
        slot = lax.rem(2 * f, slots)
        down = dot_tn(act, cot)
        up = dot(turned_v[:, at], back_up)

        @pl.when(tok == 0)
        def _():
            grads[slot] = down
            grads[slot + 1] = up

        @pl.when(tok > 0)
        def _():
            grads[slot] = grads[slot] + down
            grads[slot + 1] = grads[slot + 1] + up

    per = total // big
    turns = inner // UNIT

    def feed_one(f, carry):
        for half in range(2):
            def one(tok, inner_carry):
                feed(f, tok)
                return inner_carry

            lax.fori_loop(half * per // 2, (half + 1) * per // 2, one, 0)
            if half == 1:
                put_units(2 * f, 2)
            tick(2 * f - 1 + half)
        return carry

    lax.fori_loop(0, turns, feed_one, 0)

    def stage_copy(buffer, target, b):
        slot = lax.rem(b, 2)
        return pltpu.make_async_copy(buffer.at[slot], target.at[:, pl.ds(pl.multiple_of(b * block, block), block), :], stage_sems.at[slot])

    def finish_two(b, carry):
        norm_sum, cot_sum = carry
        at = at_block(b)

        @pl.when(b >= 2)
        def _():
            stage_copy(mixed_s, mixed_out, b - 2).wait()
        mixed = jnp.swapaxes(mixed_v[at].reshape(block, rows, width), 0, 1)
        mixed_s[lax.rem(b, 2)] = mixed.astype(BF16)
        stage_copy(mixed_s, mixed_out, b).start()
        value, grad, cot = middle_v[at], second_v[at], cot_v[at].astype(F32)
        scale = lax.rsqrt(jnp.mean(value * value, axis=-1, keepdims=True) + EPS)
        plain = value * scale
        norm_sum = norm_sum + jnp.sum((grad * plain).reshape(size // 8, 8, width), axis=0)
        cot_sum = cot_sum + jnp.sum(cot.reshape(size // 8, 8, width), axis=0)
        lean = grad * gains
        back = cot + scale * (lean - plain * jnp.mean(lean * plain, axis=-1, keepdims=True))
        second_v[at] = back
        low_v[at] = back.astype(BF16)
        return norm_sum, cot_sum

    zero = jnp.zeros((8, width), F32)
    norm_sum, cot_sum = lax.fori_loop(0, blocks, finish_two, (zero, zero))
    for b in (blocks - 2, blocks - 1):
        stage_copy(mixed_s, mixed_out, b).wait()
    put_small(20, jnp.sum(norm_sum, axis=0, keepdims=True))
    put_small(24, sums_v[0:1])
    put_small(40, jnp.sum(cot_sum, axis=0, keepdims=True))
    tick(2 * turns - 1)

    loads[4].wait()
    loads[5].wait()

    def stream(buffer, source, j, b, k):
        slot = lax.rem(b, 2)
        lanes = pl.ds(j * wide, wide)
        return pltpu.make_async_copy(source.at[at_block(b), lanes], buffer.at[slot], stream_sems.at[k, slot])

    flows = [mixed_v, flow_v]

    def first_pass(j):
        stream(decay_s, decay_in, j, blocks - 1, 0).start()

        def one(i, carry):
            product, flow = carry
            b = blocks - 1 - i
            at = at_block(b)

            @pl.when(b > 0)
            def _():
                stream(decay_s, decay_in, j, b - 1, 0).start()
            back = dot_nt(low_v[at], w_out_v[pl.ds(j * wide, wide)])
            flows[j][at] = back
            stream(decay_s, decay_in, j, b, 0).wait()
            slot = lax.rem(b, 2)
            for t in reversed(range(block)):
                here = slice(t * rows, (t + 1) * rows)
                decay = decay_s[slot, here]
                flow = decay * (back[here] + flow)
                product = decay * product
            return product, flow

        product, flow = lax.fori_loop(0, blocks, one, (jnp.ones((rows, wide), F32), jnp.zeros((rows, wide), F32)))
        chain.start(j, product, flow)

    def grad_out(j):
        slot = (2 * turns + j) % slots

        def one(tok, carry):
            at = at_block(tok, big)
            part = dot_tn(state_v[at, pl.ds(j * UNIT, UNIT)], low_v[at])

            @pl.when(tok == 0)
            def _():
                grads[slot] = part

            @pl.when(tok > 0)
            def _():
                grads[slot] = grads[slot] + part
            return carry

        lax.fori_loop(0, per, one, 0)
        put_units(2 * turns + j, 1)

    now = 2 * turns
    for j in range(halves):
        first_pass(j)
        grad_out(j)
        for i in range(j):
            if j - 1 - i < chain.rounds:
                chain.advance(i, j - 1 - i)
        tick(now)
        now += 1

    loads[7].wait()
    gains_one = gain_one[...]

    def norm_one(b, carry):
        at = at_block(b)
        value = x_v[at].astype(F32)
        scale = lax.rsqrt(jnp.mean(value * value, axis=-1, keepdims=True) + EPS)
        turned_v[:, at] = jnp.swapaxes(value * scale * gains_one, 0, 1).astype(BF16)
        middle_v[at] = jnp.zeros_like(value)
        return carry

    streams = ((decay_s, decay_in), (fade_s, fade_in), (rise_s, rise_in), (weight_s, weight_in), (lean_s, lean_in))
    backs = [lambda at: (state_v, (at, slice(0, UNIT))), lambda at: (state_v, (at, slice(UNIT, 2 * UNIT))), lambda at: (cot_v, (at, slice(None)))]

    def second_pass(j):
        for k, (buffer, source) in enumerate(streams):
            stream(buffer, source, j, blocks - 1, k).start()

        def one(i, carry):
            flow, sum_f, sum_i = carry
            b = blocks - 1 - i
            at = at_block(b)
            slot = lax.rem(b, 2)

            @pl.when(b > 0)
            def _():
                for k, (buffer, source) in enumerate(streams):
                    stream(buffer, source, j, b - 1, k).start()
            for k, (buffer, source) in enumerate(streams):
                stream(buffer, source, j, b, k).wait()
            parts = []
            for t in reversed(range(block)):
                here = slice(t * rows, (t + 1) * rows)
                there = pl.ds(pl.multiple_of(b * size + t * rows, rows), rows)
                reach = flows[j][there] + flow
                flow = decay_s[slot, here] * reach
                lean = reach * lean_s[slot, here].astype(F32)
                grad_f = fade_s[slot, here].astype(F32) * lean
                grad_i = -(rise_s[slot, here].astype(F32) * lean)
                sum_f, sum_i = sum_f + grad_f, sum_i + grad_i
                state_v[there, 0:UNIT] = grad_f.astype(BF16)
                state_v[there, UNIT : 2 * UNIT] = grad_i.astype(BF16)
                cot_v[there] = (weight_s[slot, here].astype(F32) * reach).astype(BF16)
            return flow, sum_f, sum_i

        none = jnp.zeros((rows, wide), F32)
        unused, sum_f, sum_i = lax.fori_loop(0, blocks, one, (join[j, 1], none, none))
        put_small(4 + 4 * j, jnp.sum(sum_f, axis=0, keepdims=True))
        put_small(12 + 4 * j, jnp.sum(sum_i, axis=0, keepdims=True))

    def project(j, k, base):
        slot = (base + k) % slots

        def one(tok, carry):
            at = at_block(tok, big)
            ref, index = backs[k](at)
            piece = ref[index]
            part = dot(turned_v[:, at], piece)
            columns = pl.ds(k * hidden + j * wide, wide)
            middle_v[at] = middle_v[at] + dot_nt(piece, w_in_v[:, columns])

            @pl.when(tok == 0)
            def _():
                grads[slot] = part

            @pl.when(tok > 0)
            def _():
                grads[slot] = grads[slot] + part
            return carry

        lax.fori_loop(0, per, one, 0)
        put_units(base + k, 1)

    base = 2 * turns + halves
    lax.fori_loop(0, blocks, norm_one, 0)
    for step in range(halves, halves + chain.rounds):
        for i in range(halves):
            if 0 <= step - 1 - i < chain.rounds:
                chain.advance(i, step - 1 - i)
    tick(now)
    now += 1
    loads[6].wait()
    for j in range(halves):
        second_pass(j)
        tick(now)
        now += 1
        for k in range(3):
            project(j, k, base + 3 * j)
            if k < 2 or j == 0:
                tick(now)
                now += 1

    def finish_one(b, norm_sum):
        at = at_block(b)

        @pl.when(b >= 2)
        def _():
            stage_copy(tokens_s, tokens_out, b - 2).wait()
        value, grad = x_v[at].astype(F32), middle_v[at]
        scale = lax.rsqrt(jnp.mean(value * value, axis=-1, keepdims=True) + EPS)
        plain = value * scale
        norm_sum = norm_sum + jnp.sum((grad * plain).reshape(size // 8, 8, width), axis=0)
        lean = grad * gains_one
        back = second_v[at] + scale * (lean - plain * jnp.mean(lean * plain, axis=-1, keepdims=True))
        tokens_s[lax.rem(b, 2)] = jnp.swapaxes(back.reshape(block, rows, width), 0, 1)
        stage_copy(tokens_s, tokens_out, b).start()
        return norm_sum

    norm_sum = lax.fori_loop(0, blocks, finish_one, jnp.zeros((8, width), F32))
    put_small(0, jnp.sum(norm_sum, axis=0, keepdims=True))
    if ringed:
        def drain(t, carry):
            tick(t)
            return carry

        lax.fori_loop(now, units + len(holes) + STAGES, drain, 0)
    else:
        copy = pltpu.make_async_copy(small_v, small_out.at[0], load_sems.at[0])
        copy.start()
        copy.wait()
    for b in (blocks - 2, blocks - 1):
        stage_copy(tokens_s, tokens_out, b).wait()
    for j in range(halves):
        chain.finish(j)


def back(ringed, shape_in, x, cot, middle, state, decay, fade, rise, weight, lean, gain_one, gain_two, up_bias, down_bias, w_in, w_out, w_up, w_down, cid=2):
    rows, steps, width = shape_in
    total = rows * steps
    hidden = w_out.shape[0]
    inner = w_down.shape[0]
    count = lax.axis_size("seq")
    block = 16
    size = block * rows
    wide = UNIT
    halves = hidden // wide
    units = 2 * (inner // UNIT) + halves + 3 * halves
    slots = 10
    first = 2 * (inner // UNIT) + halves
    holes = (first, first + 1, first + 5)
    anywhere = pl.BlockSpec(memory_space=pl.ANY)
    vmem = pl.BlockSpec(memory_space=pltpu.VMEM)
    shape = jax.ShapeDtypeStruct
    if ringed:
        more = sum_scratch(units, slots, UNIT, width) + sum_scratch(1, 1, SMALL_ROWS, 128)
    else:
        more = [pltpu.VMEM((slots, UNIT, width), F32), pltpu.VMEM((1, SMALL_ROWS, 128), F32)]
    return pl.pallas_call(
        functools.partial(back_kernel, ringed, count, rows, steps, units, slots, holes, block),
        out_shape=(
            shape(shape_in, BF16), shape(shape_in, F32), shape((units, UNIT, width), F32), shape((1, SMALL_ROWS, 128), F32),
        ),
        in_specs=[anywhere] * 9 + [vmem] * 4 + [anywhere] * 4,
        out_specs=(anywhere,) * 4,
        scratch_shapes=[
            pltpu.VMEM((total, width), F32), pltpu.VMEM((total, width), F32), pltpu.VMEM((total, width), F32), pltpu.VMEM((total, width), F32),
            pltpu.VMEM((total, hidden), BF16), pltpu.VMEM((total, width), BF16), pltpu.VMEM((total, width), BF16), pltpu.VMEM((total, width), BF16),
            pltpu.VMEM((width, total), BF16),
            pltpu.VMEM(w_in.shape, BF16), pltpu.VMEM(w_out.shape, BF16), pltpu.VMEM(w_up.shape, BF16), pltpu.VMEM(w_down.shape, BF16),
            pltpu.VMEM((2, size, wide), F32), pltpu.VMEM((2, size, wide), BF16), pltpu.VMEM((2, size, wide), BF16),
            pltpu.VMEM((2, size, wide), BF16), pltpu.VMEM((2, size, wide), BF16),
            pltpu.VMEM((2, rows, block, width), BF16), pltpu.VMEM((2, rows, block, width), F32), pltpu.VMEM((8, inner), F32),
            pltpu.SemaphoreType.DMA((8,)), pltpu.SemaphoreType.DMA((5, 2)), pltpu.SemaphoreType.DMA((2,)),
            *chain_scratch(halves, count, rows, wide),
            *more,
        ],
        compiler_params=pltpu.CompilerParams(collective_id=cid, has_side_effects=True, vmem_limit_bytes=63 * 2**20),
        cost_estimate=pl.CostEstimate(flops=2 * total * width * (8 * hidden + 6 * inner), bytes_accessed=80 * 2**20, transcendentals=total * inner),
        name="back",
    )(x, cot, middle, state, decay, fade, rise, weight, lean, gain_one.reshape(1, -1), gain_two.reshape(1, -1), up_bias.reshape(1, -1), down_bias.reshape(1, -1), w_in, w_out, w_up, w_down)


def on_device(tokens, cotangent, reset_pos, norm1_gain, w_in, forget_bias, input_bias, w_out, norm2_gain, w_up, up_bias, w_down, down_bias):
    ringed = lax.axis_size("seq") == 8 and lax.axis_size("rows") == 4
    width = tokens.shape[-1]
    hidden, inner = w_out.shape[0], w_down.shape[0]
    kept = front(tokens, cotangent, reset_pos, norm1_gain, w_in, forget_bias, input_bias, w_out)
    mixed, grad_tokens, units, small = back(
        ringed, tokens.shape, *kept, norm1_gain, norm2_gain, up_bias, down_bias, w_in, w_out, w_up, w_down
    )
    if not ringed:
        units, small = lax.psum((units, small), ("seq", "rows"))
    feeds = inner // UNIT
    halves = hidden // UNIT
    grad_down = jnp.concatenate([units[2 * f] for f in range(feeds)], axis=0)
    grad_up = jnp.concatenate([units[2 * f + 1] for f in range(feeds)], axis=1)
    grad_out = units[2 * feeds : 2 * feeds + halves].reshape(hidden, width)
    base = 2 * feeds + halves
    grad_in = jnp.concatenate([units[base + 3 * j + k] for k in range(3) for j in range(halves)], axis=1)
    flat = small[0]

    def rows_of(first, length):
        return flat[first : first + length // 128].reshape(length)

    return (
        mixed, grad_tokens, rows_of(0, width), grad_in, rows_of(4, hidden), rows_of(12, hidden), grad_out,
        rows_of(20, width), grad_up, rows_of(24, inner), grad_down, rows_of(40, width),
    )


def solution(mesh):
    return jax.shard_map(
        on_device,
        mesh=mesh,
        in_specs=(
            P("rows", "seq", None),
            P("rows", "seq", None),
            P("rows", None),
            P(),
            P(),
            P(),
            P(),
            P(),
            P(),
            P(),
            P(),
            P(),
            P(),
        ),
        out_specs=(
            P("rows", "seq", None),
            P("rows", "seq", None),
            P(),
            P(),
            P(),
            P(),
            P(),
            P(),
            P(),
            P(),
            P(),
            P(),
        ),
        check_vma=False,
    )
```

time: 877 us -> 292 us (0.33); the launches traced: 861 us -> 291 us
  other arithmetic: 274 us -> 6.8 us
  blocking collectives: 167 us -> 0 us
  matrix products: 130 us -> 0 us
  local copies, waits for them, and re-layouts: 126 us -> 31.1 us
  Pallas kernels: 159 us -> 253 us
    dot_general x18 -> x0, matrix products: 130 us -> none  [the longest x6 37.1 us: right_dot(): lax.dot_general(left, right, (((1,), (1,)), ((), ())), preferred_element_...]
    all_gather x4 -> x0, blocking collectives: 127 us -> none  [carried_in(): gathered = jax.tree.map(lambda a: lax.all_gather(a, axis), part)]
    while x112 -> x0, other arithmetic: 107 us -> none
    pallas_call x1 -> x2, Pallas kernels: 159 us -> 253 us  [the longest x1 217 us: back(): pl.pallas_call(functools.partial(back_kernel, ringed, count, rows, steps,...]
    mul x34 -> x0, other arithmetic: 53.1 us -> none  [the longest x16 21.4 us: back_summary(): flowing = decay_piece[offset] * (back_piece[offset] + flowing)]
    another operation x48 -> x0, other arithmetic: 42.5 us -> none  [the longest x32 28.7 us: state_step(): return (running, (jnp.stack(states_out), jnp.stack(before_out)))]
    psum x1 -> x0, blocking collectives: 40.2 us -> none  [on_device(): lax.psum((grad_norm1, grad_forget, grad_input, grad_norm2, grad_up_bias,...]
    dynamic_update_slice x48 -> x0, local copies, waits for them, and re-layouts: 38.7 us -> none  [on_device(): lax.scan(state_step, carried, (decay_blocks, update_blocks))]
where the time goes in v2:
time: 292 us; the launch traced here: 291 us
  Pallas kernels  253 us (87%)
  local copies, waits for them, and re-layouts  31.1 us (11%)
  other arithmetic  6.8 us (2%)
    pallas_call x1, Pallas kernels, back(): pl.pallas_call(functools.partial(back_kernel, ringed, count, rows, steps,...  217 us
    pallas_call x1, Pallas kernels, front(): pl.pallas_call(functools.partial(front_kernel, count, rows, steps, chunk,...  35.5 us
    unnamed x14, local copies, waits for them, and re-layouts  19 us

profile of v2, /device:TPU:0, one launch (start us, length us, event | category | flops | bytes accessed | tf_op | source)
XLA Modules:
  0.0 291.4 jit_solution(9219859117982929429)
XLA Ops:
  0.6 1.4 copy.25.reset
  2.0 35.5 %front.1 = (bf16[2048,512]{1,0:T(8,128)(2,1)}, bf16[2048,512]{1,0:T(8,128)(2,1)}, f32[2048,512]{1,0:T(8,128)}, bf16[2048,1024]{1,0:T(8,128)(2,1)}, f32[2048,1024...) custom-call(bf16[16,128,512]{2,1,0:T(8,128)(2,1)} %tokens.1, ...), custom_call_target="tpu_custom_call" | custom-call | flops 8589934592 | bytes 41943040 | tf_op jit(solution)/shard_map/front/pallas_call | solution.py:311
  37.5 217.3 %back.1 = (bf16[16,128,512]{2,1,0:T(8,128)(2,1)}, f32[16,128,512]{2,1,0:T(8,128)}, f32[16,512,512]{2,1,0:T(8,128)}, f32[1,256,128]{2,1,0:T(8,128)}) custom-call(bf16[2048,512]{1,0:T(8,128)(2,1)} %get-tuple-element.25.x_in, bf16[2048,512]{1,0:T(8,128)(2,1)} %get-tuple-element.26.cot_in, f32[2048,512]{1,0:T(8,128)} %get-tuple-element.27.middle_in, ...), custom_call_target="tpu_custom_call" | custom-call | flops 42949672960 | bytes 83886080 | tf_op jit(solution)/shard_map/back/pallas_call | solution.py:939
  254.8 1.3 slice_bitcast_fusion.11
  256.1 1.3 slice_bitcast_fusion.8
  257.4 1.4 slice_bitcast_fusion.9
  258.8 0.0 copy-start
  258.8 3.2 %slice.78 = f32[2,512,512]{2,1,0:T(8,128)} slice(f32[16,512,512]{2,1,0:T(8,128)} %get-tuple-element.37), slice={[8:10], [0:512], [0:512]} | slice | bytes 4194304 | tf_op jit(solution)/shard_map/slice | solution.py:978
  262.0 3.0 %bitcast_dynamic-update-slice_fusion.5 = f32[512,3072]{1,0:T(8,128)} fusion(f32[16,512,512]{2,1,0:T(8,128)} %get-tuple-element.37), kind=kLoop, calls=%fused_computation.7 | loop fusion | bytes 2097152
  265.0 2.9 bitcast_dynamic-update-slice_fusion.4
  267.9 2.3 bitcast_dynamic-update-slice_fusion.3
  270.2 2.3 bitcast_dynamic-update-slice_fusion.2
  272.4 2.3 bitcast_dynamic-update-slice_fusion.1
  274.7 2.3 bitcast_dynamic-update-slice_fusion
  277.0 0.0 copy-done
  277.0 2.7 slice_bitcast_fusion.3
  279.6 4.4 %pad_maximum_fusion.1 = f32[2048,512]{1,0:T(8,128)} fusion(f32[512,512]{1,0:T(8,128)} %get-tuple-element.39, f32[512,512]{1,0:T(8,128)} %get-tuple-element.40, f32[512,512]{1,0:T(8,128)} %get-tuple-element.41, f32[512,512]{1,0:T(8,128)S(1)} %get-tuple-element.38), kind=kLoop, calls=%fused_computation.1 | loop fusion | flops 3145728 | bytes 8388608 | tf_op jit(solution)/shard_map/concatenate | solution.py:976
  284.1 0.0 copy-start.2
  284.1 2.4 pad_maximum_fusion
  286.4 0.0 copy-done.2
  286.5 0.0 copy-start.1
  286.5 1.3 copy.33
  287.8 1.6 copy-done.1
  289.4 2.0 copy.34
Async XLA Ops:
  258.8 18.2 %copy-start = (f32[16,512,512]{2,1,0:T(8,128)S(1)}, f32[16,512,512]{2,1,0:T(8,128)}, u32[]{:S(2)}) copy-start(f32[16,512,512]{2,1,0:T(8,128)} %get-tuple-element.37) | copy-start | bytes 50331652
  284.1 2.4 copy-start.2
  286.5 2.9 %copy-start.1 = (f32[16,128,512]{2,1,0:T(8,128)S(1)}, f32[16,128,512]{2,1,0:T(8,128)}, u32[]{:S(2)}) copy-start(f32[16,128,512]{2,1,0:T(8,128)} %get-tuple-element.64) | copy-start | bytes 12582916

commit v3 on v2

--- a/solution.py
+++ b/solution.py
@@ -12,7 +12,15 @@
 F32 = jnp.float32
 BF16 = jnp.bfloat16
 STAGES = 13
-KINDS = 14
+KINDS = 10
+SPAN = 512
+UNIT = 256
+WIDE = 512
+SLOTS = 12
+SMALL_ROWS = 48
+DOUBLINGS = 5
+SLOW = (0, 1, 3, 6, 8, 10, 11, 12, 14, 16, 19, 21, 22)
+FAST = (0, 1, 3, 5, 7, 8, 9, 10, 11, 13, 15, 17, 18)
 
 
 def place():
@@ -333,8 +341,8 @@
 
 
 class Summing:
-    def __init__(self, span, grads, slots, half_in, part_in, up_in, down_in, last_in, result, send, recv, local):
-        self.grads, self.slots = grads, slots
+    def __init__(self, plan, grads, half_in, part_in, up_in, down_in, last_in, send, recv, local, result):
+        self.plan, self.grads = plan, grads
         self.half_in, self.part_in, self.up_in, self.down_in, self.last_in = half_in, part_in, up_in, down_in, last_in
         self.result, self.send, self.recv, self.local = result, send, recv, local
         x, y, z, core = place()
@@ -348,7 +356,7 @@
         self.below = spot(x, y, z - 1, core)
         near_bit = jnp.where(first, x, y)
         far_bit = jnp.where(first, y, x)
-        self.n_half, self.n_part, self.n_line, self.n_tip = span // 2, span // 4, span // 16, span // 32
+        self.n_half, self.n_part, self.n_line, self.n_tip = SPAN // 2, SPAN // 4, SPAN // 16, SPAN // 32
         self.half = core * self.n_half
         self.other_half = (1 - core) * self.n_half
         self.part = self.half + near_bit * self.n_part
@@ -362,65 +370,74 @@
             device_id=device, device_id_type=MESH,
         )
 
-    def rows(self, unit, start, count):
-        return self.grads.at[lax.rem(unit, self.slots), pl.ds(pl.multiple_of(start, 8), count)]
-
-    def done(self, unit, start, count):
-        return self.result.at[unit, pl.ds(pl.multiple_of(start, 8), count)]
+    def slot_of(self, u):
+        return self.plan[u] if isinstance(u, int) else (u, 0, WIDE)
+
+    def rows(self, u, start, count):
+        slot, column, width = self.slot_of(u)
+        return self.grads.at[slot, pl.ds(pl.multiple_of(start, 8), count), pl.ds(column, width)]
+
+    def done(self, u, start, count):
+        return self.result.at[u, pl.ds(pl.multiple_of(start, 8), count), pl.ds(0, self.slot_of(u)[2])]
+
+    def land(self, ref, u, slots, start, count):
+        return ref.at[lax.rem(u, slots), pl.ds(start, count), pl.ds(0, self.slot_of(u)[2])]
 
     def c_half(self, u):
-        return self.copy(0, u, self.rows(u, self.other_half, self.n_half), self.half_in.at[lax.rem(u, 2)], self.sibling)
+        return self.copy(0, u, self.rows(u, self.other_half, self.n_half), self.land(self.half_in, u, 4, 0, self.n_half), self.sibling)
 
     def c_part(self, u):
-        return self.copy(1, u, self.rows(u, self.other_part, self.n_part), self.part_in.at[lax.rem(u, 2)], self.near)
+        return self.copy(1, u, self.rows(u, self.other_part, self.n_part), self.land(self.part_in, u, 4, 0, self.n_part), self.near)
 
     def c_up(self, u, z):
         low, rest = self.n_line * (z + 1), self.n_line * (3 - z)
-        return self.copy(2, u, self.rows(u, self.part + low, rest), self.up_in.at[lax.rem(u, 4), pl.ds(low - self.n_line, rest)], self.above)
+        return self.copy(2, u, self.rows(u, self.part + low, rest), self.land(self.up_in, u, 8, low - self.n_line, rest), self.above)
 
     def c_down(self, u, z):
         rest = self.n_line * z
-        return self.copy(3, u, self.rows(u, self.part, rest), self.down_in.at[lax.rem(u, 4), pl.ds(0, rest)], self.below)
+        return self.copy(3, u, self.rows(u, self.part, rest), self.land(self.down_in, u, 8, 0, rest), self.below)
 
     def c_last(self, u):
-        return self.copy(4, u, self.rows(u, self.other_tip, self.n_tip), self.last_in.at[u], self.far)
+        return self.copy(4, u, self.rows(u, self.other_tip, self.n_tip), self.last_in.at[u, :, pl.ds(0, self.slot_of(u)[2])], self.far)
 
     def c_own(self, u):
         return pltpu.make_async_copy(self.rows(u, self.tip, self.n_tip), self.done(u, self.tip, self.n_tip), self.local.at[u])
 
-    def c_far(self, u):
-        return self.copy(5, u, self.rows(u, self.tip, self.n_tip), self.done(u, self.tip, self.n_tip), self.far)
-
-    def c_rise(self, u, hop, back=0):
-        piece = self.done(u, self.part + self.n_line * (self.z - hop - back), self.n_line)
-        return self.copy(6 + hop, u, piece, piece, self.above)
-
-    def c_fall(self, u, hop, back=0):
-        piece = self.done(u, self.part + self.n_line * (self.z + hop + back), self.n_line)
-        return self.copy(9 + hop, u, piece, piece, self.below)
+    def c_far(self, u, start):
+        return self.copy(5, u, self.rows(u, start, self.n_tip), self.done(u, start, self.n_tip), self.far)
+
+    def c_rise(self, u, z):
+        piece = self.done(u, self.part, self.n_line * (z + 1))
+        return self.copy(6, u, piece, piece, self.above)
+
+    def c_fall(self, u, z):
+        piece = self.done(u, self.part + self.n_line * z, self.n_line * (4 - z))
+        return self.copy(7, u, piece, piece, self.below)
 
     def c_near(self, u, start):
         piece = self.done(u, start, self.n_part)
-        return self.copy(12, u, piece, piece, self.near)
+        return self.copy(8, u, piece, piece, self.near)
 
     def c_sibling(self, u, start):
         piece = self.done(u, start, self.n_half)
-        return self.copy(13, u, piece, piece, self.sibling)
+        return self.copy(9, u, piece, piece, self.sibling)
 
     def add(self, u, start, count, ref):
-        slot = lax.rem(u, self.slots)
-        step = math.gcd(count, 32)
+        slot, column, width = self.slot_of(u)
+        step = math.gcd(count, 64)
+        lanes = pl.ds(column, width)
 
         def one(i, carry):
             here = pl.ds(pl.multiple_of(start + i * step, 8), step)
             there = pl.ds(pl.multiple_of(i * step, 8), step)
-            self.grads[slot, here] = self.grads[slot, here] + ref[there]
+            self.grads[slot, here, lanes] = self.grads[slot, here, lanes] + ref[there]
             return carry
 
-        if count == step:
-            one(0, 0)
-        else:
-            lax.fori_loop(0, count // step, one, 0)
+        lax.fori_loop(0, count // step, one, 0)
+
+    def at_each(self, action):
+        for k in range(4):
+            pl.when(self.z == k)(functools.partial(action, k))
 
     def stage(self, s, u):
         z = self.z
@@ -428,77 +445,75 @@
             self.c_half(u).start()
         elif s == 1:
             self.c_half(u).wait()
-            self.add(u, self.half, self.n_half, self.half_in.at[lax.rem(u, 2)])
+            self.add(u, self.half, self.n_half, self.land(self.half_in, u, 4, 0, self.n_half))
             self.c_part(u).start()
         elif s == 2:
             self.c_part(u).wait()
-            self.add(u, self.part, self.n_part, self.part_in.at[lax.rem(u, 2)])
+            self.add(u, self.part, self.n_part, self.land(self.part_in, u, 4, 0, self.n_part))
         if 2 <= s <= 5:
-            for k in range(4):
-                if s == 2 + k:
-                    @pl.when(z == k)
-                    def _():
-                        if k > 0:
-                            self.c_up(u, k - 1).wait_recv()
-                            low, rest = self.n_line * k, self.n_line * (4 - k)
-                            self.add(u, self.part + low, rest, self.up_in.at[lax.rem(u, 4), pl.ds(low - self.n_line, rest)])
-                        if k < 3:
-                            self.c_up(u, k).start()
-                if s == 5 - k:
-                    @pl.when(z == k)
-                    def _():
-                        if k < 3:
-                            self.c_down(u, k + 1).wait_recv()
-                            rest = self.n_line * (k + 1)
-                            self.add(u, self.part, rest, self.down_in.at[lax.rem(u, 4), pl.ds(0, rest)])
-                        if k > 0:
-                            self.c_down(u, k).start()
+            up, down = s - 2, 5 - s
+
+            @pl.when(z == up)
+            def _():
+                if up > 0:
+                    self.c_up(u, up - 1).wait_recv()
+                    low, rest = self.n_line * up, self.n_line * (4 - up)
+                    self.add(u, self.part + low, rest, self.land(self.up_in, u, 8, low - self.n_line, rest))
+                if up < 3:
+                    self.c_up(u, up).start()
+
+            @pl.when(z == down)
+            def _():
+                if down < 3:
+                    self.c_down(u, down + 1).wait_recv()
+                    rest = self.n_line * (down + 1)
+                    self.add(u, self.part, rest, self.land(self.down_in, u, 8, 0, rest))
+                if down > 0:
+                    self.c_down(u, down).start()
         if s == 5:
             self.c_last(u).start()
         elif s == 6:
-            for k in range(4):
-                @pl.when(z == k)
-                def _():
-                    if k < 3:
-                        self.c_up(u, k).wait_send()
-                    if k > 0:
-                        self.c_down(u, k).wait_send()
+            def sent(k):
+                if k < 3:
+                    self.c_up(u, k).wait_send()
+                if k > 0:
+                    self.c_down(u, k).wait_send()
+
+            self.at_each(sent)
             self.c_last(u).wait()
-            self.add(u, self.tip, self.n_tip, self.last_in.at[u])
-            self.c_far(u).start()
+            self.add(u, self.tip, self.n_tip, self.last_in.at[u, :, pl.ds(0, self.slot_of(u)[2])])
+            self.c_far(u, self.tip).start()
             self.c_own(u).start()
         elif s == 7:
-            self.c_far(u).wait()
+            self.c_far(u, self.tip).wait_send()
+            self.c_far(u, self.other_tip).wait_recv()
             self.c_own(u).wait()
         if 7 <= s <= 10:
-            hop = s - 7
-            if hop > 0:
-                @pl.when(z >= hop)
-                def _():
-                    self.c_rise(u, hop - 1, 1).wait_recv()
-
-                @pl.when(z + hop < 4)
-                def _():
-                    self.c_fall(u, hop - 1, 1).wait_recv()
-            if hop < 3:
-                @pl.when((z >= hop) & (z < 3))
-                def _():
-                    self.c_rise(u, hop).start()
-
-                @pl.when((z + hop < 4) & (z > 0))
-                def _():
-                    self.c_fall(u, hop).start()
+            up, down = s - 7, 10 - s
+
+            @pl.when(z == up)
+            def _():
+                if up > 0:
+                    self.c_rise(u, up - 1).wait_recv()
+                if up < 3:
+                    self.c_rise(u, up).start()
+
+            @pl.when(z == down)
+            def _():
+                if down < 3:
+                    self.c_fall(u, down + 1).wait_recv()
+                if down > 0:
+                    self.c_fall(u, down).start()
         if s == 10:
             self.c_near(u, self.part).start()
         elif s == 11:
-            for hop in range(3):
-                @pl.when((z >= hop) & (z < 3))
-                def _():
-                    self.c_rise(u, hop).wait_send()
-
-                @pl.when((z + hop < 4) & (z > 0))
-                def _():
-                    self.c_fall(u, hop).wait_send()
+            def sent(k):
+                if k < 3:
+                    self.c_rise(u, k).wait_send()
+                if k > 0:
+                    self.c_fall(u, k).wait_send()
+
+            self.at_each(sent)
             self.c_near(u, self.part).wait_send()
             self.c_near(u, self.other_part).wait_recv()
             self.c_sibling(u, self.half).start()
@@ -507,20 +522,43 @@
             self.c_sibling(u, self.other_half).wait_recv()
 
 
-def sum_scratch(units, slots, span, width):
+def sum_scratch(units, slots):
     return [
-        pltpu.VMEM((slots, span, width), F32),
-        pltpu.VMEM((2, span // 2, width), F32),
-        pltpu.VMEM((2, span // 4, width), F32),
-        pltpu.VMEM((4, 3 * span // 16, width), F32),
-        pltpu.VMEM((4, 3 * span // 16, width), F32),
-        pltpu.VMEM((units, span // 32, width), F32),
+        pltpu.VMEM((slots, SPAN, WIDE), F32),
+        pltpu.VMEM((4, SPAN // 2, WIDE), F32),
+        pltpu.VMEM((4, SPAN // 4, WIDE), F32),
+        pltpu.VMEM((8, 3 * SPAN // 16, WIDE), F32),
+        pltpu.VMEM((8, 3 * SPAN // 16, WIDE), F32),
+        pltpu.VMEM((units, SPAN // 32, WIDE), F32),
         pltpu.SemaphoreType.DMA((KINDS, units)),
         pltpu.SemaphoreType.DMA((KINDS, units)),
         pltpu.SemaphoreType.DMA((units,)),
     ]
 
 
+class Doubling:
+    def __init__(self, own, got, send, recv):
+        self.own, self.got, self.send, self.recv = own, got, send, recv
+        x, y, z, core = place()
+        self.partners = (
+            spot(x, y, z, 1 - core), spot(1 - x, y, z, core), spot(x, 1 - y, z, core),
+            spot(x, y, z + 1 - 2 * lax.rem(z, 2), core), spot(x, y, z + 2 - 4 * lax.div(z, 2), core),
+        )
+
+    def copy(self, k):
+        return pltpu.make_async_remote_copy(
+            src_ref=self.own.at[k], dst_ref=self.got.at[k], send_sem=self.send.at[k], recv_sem=self.recv.at[k],
+            device_id=self.partners[k], device_id_type=MESH,
+        )
+
+    def step(self, k):
+        if k > 0:
+            self.copy(k - 1).wait()
+            self.own[k] = self.own[k - 1] + self.got[k - 1]
+        if k < DOUBLINGS:
+            self.copy(k).start()
+
+
 def greet_ring(ring):
     barrier = pltpu.get_barrier_semaphore()
     for there in (ring.sibling, ring.near, ring.far):
@@ -539,16 +577,14 @@
 
 GELU_A = math.sqrt(2.0 / math.pi)
 GELU_B = GELU_A * 0.044715
-UNIT = 512
-SMALL_ROWS = 256
 
 
 def back_kernel(
-    ringed, count, rows, steps, units, slots, holes, block,
+    ringed, count, rows, steps, plan, block,
     x_in, cot_in, middle_in, state_in, decay_in, fade_in, rise_in, weight_in, lean_in,
     gain_one, gain_two, up_bias, down_bias, w_in, w_out, w_up, w_down,
     mixed_out, tokens_out, result, small_out,
-    middle_v, second_v, mixed_v, flow_v, state_v, cot_v, x_v, low_v, turned_v, w_in_v, w_out_v, w_up_v, w_down_v,
+    middle_v, second_v, mixed_v, state_v, cot_v, x_v, low_v, cand_v, turned_v, w_in_v, w_out_v, w_up_v, w_down_v,
     decay_s, fade_s, rise_s, weight_s, lean_s, mixed_s, tokens_s, sums_v,
     load_sems, stream_sems, stage_sems,
     sent, got, join, send, recv,
@@ -560,18 +596,18 @@
     size = block * rows
     blocks = steps // block
     wide = UNIT
-    halves = hidden // wide
+    parts = hidden // wide
     big = 512
+    per = total // big
+    feeds = inner // SPAN
     chain = Chain(count, -1, sent, got, join, send, recv)
     barrier, greeted = greet_chain(chain)
-    grads = ring_refs[0]
+    grads, own_v = ring_refs[:2]
     if ringed:
-        ring = Summing(UNIT, grads, slots, *ring_refs[1:6], result, *ring_refs[6:9])
-        small = Summing(SMALL_ROWS, ring_refs[9], 1, *ring_refs[10:15], small_out, *ring_refs[15:18])
+        ring = Summing(plan, grads, *ring_refs[2:10], result)
+        small = Doubling(own_v, *ring_refs[10:])
         greeted = greeted + greet_ring(ring)
-        small_v = ring_refs[9].at[0]
-    else:
-        small_v = ring_refs[1].at[0]
+    small_v = own_v.at[0]
 
     loads = [
         pltpu.make_async_copy(source, target, load_sems.at[k])
@@ -586,37 +622,44 @@
     def at_block(b, n=size):
         return pl.ds(pl.multiple_of(b * n, n), n)
 
-    def stage_at(t, s):
-        v = t - s
-        if isinstance(v, int):
-            u = v - sum(hole < v for hole in holes)
-            if 0 <= v and v not in holes and u <= units:
-                ring.stage(s, u) if u < units else small.stage(s, 0)
-            return
-        u, real = v, v >= 0
-        for hole in holes:
-            u = u - jnp.where(v > hole, 1, 0)
-            real = real & (v != hole)
-
-        @pl.when(real & (u < units))
-        def _():
-            ring.stage(s, u)
-
-        @pl.when(real & (u == units))
-        def _():
-            small.stage(s, 0)
-
-    def tick(t):
+    flying = {}
+    waiting = []
+    clock = [0]
+
+    def pace(unit):
+        return SLOW if plan[unit][2] > UNIT else FAST
+
+    def tick():
+        now = clock[0]
+        clock[0] += 1
+        if waiting:
+            flying[waiting.pop(0)] = now
         if ringed:
-            for s in reversed(range(STAGES)):
-                stage_at(t, s)
-
-    def put_units(first, number):
+            for unit in sorted(flying):
+                if now - flying[unit] in pace(unit):
+                    ring.stage(pace(unit).index(now - flying[unit]), unit)
+
+    def rolling_tick(i, half):
+        for s in reversed(range(STAGES)):
+            behind = SLOW[s] + early - half
+            if ringed and behind % 2 == 0 and behind // 2 < feeds * per // 2:
+                pl.when(i >= behind // 2)(functools.partial(ring.stage, s, i - behind // 2))
+
+    def beat(number, body, ticks, *carry):
+        each = number // ticks
+        for k in range(ticks):
+            carry = lax.fori_loop(each * k, each * k + each, lambda i, c: body(i, *c), carry)
+            tick()
+        return carry
+
+    def put_unit(unit):
         if not ringed:
-            for k in range(number):
-                copy = pltpu.make_async_copy(grads.at[lax.rem(first + k, slots)], result.at[first + k], load_sems.at[0])
-                copy.start()
-                copy.wait()
+            slot, column, length = plan[unit] if isinstance(unit, int) else (unit, 0, WIDE)
+            copy = pltpu.make_async_copy(
+                grads.at[slot, :, pl.ds(column, length)], result.at[unit, :, pl.ds(0, length)], load_sems.at[0]
+            )
+            copy.start()
+            copy.wait()
 
     sums_v[...] = jnp.zeros_like(sums_v)
     small_v[...] = jnp.zeros_like(small_v)
@@ -624,6 +667,17 @@
     def put_small(row, value):
         for k in range(value.shape[1] // 128):
             small_v[pl.ds(row + k, 1)] = value[:, 128 * k : 128 * k + 128]
+
+    def gather(slot, column, value, fresh):
+        lanes = pl.ds(column, value.shape[1])
+
+        @pl.when(fresh)
+        def _():
+            grads[slot, :, lanes] = value
+
+        @pl.when(jnp.logical_not(fresh))
+        def _():
+            grads[slot, :, lanes] = grads[slot, :, lanes] + value
 
     loads[0].wait()
     gains = gain_two[...]
@@ -647,7 +701,7 @@
 
     def feed(f, tok):
         at = at_block(tok, big)
-        lanes = pl.ds(pl.multiple_of(f * UNIT, UNIT), UNIT)
+        lanes = pl.ds(pl.multiple_of(f * SPAN, SPAN), SPAN)
         cot = cot_v[at]
         pre = dot(low_v[at], w_up_v[:, lanes]) + up_bias[:, lanes]
         back_act = dot_nt(cot, w_down_v[lanes])
@@ -660,43 +714,33 @@
         act, back_up = act.astype(BF16), back_up.astype(BF16)
         mixed_v[at] = mixed_v[at] + dot(act, w_down_v[lanes])
         second_v[at] = second_v[at] + dot_nt(back_up, w_up_v[:, lanes])
-        slot = lax.rem(2 * f, slots)
-        down = dot_tn(act, cot)
-        up = dot(turned_v[:, at], back_up)
-
-        @pl.when(tok == 0)
-        def _():
-            grads[slot] = down
-            grads[slot + 1] = up
-
-        @pl.when(tok > 0)
-        def _():
-            grads[slot] = grads[slot] + down
-            grads[slot + 1] = grads[slot + 1] + up
-
-    per = total // big
-    turns = inner // UNIT
-
-    def feed_one(f, carry):
+        gather(2 * f, 0, dot_tn(act, cot), tok == 0)
+        gather(2 * f + 1, 0, dot(turned_v[:, at], back_up), tok == 0)
+
+    early = per - 1
+
+    def feed_pair(i, carry):
+        f, tok = lax.div(2 * i, per), lax.rem(2 * i, per)
         for half in range(2):
-            def one(tok, inner_carry):
-                feed(f, tok)
-                return inner_carry
-
-            lax.fori_loop(half * per // 2, (half + 1) * per // 2, one, 0)
+            feed(f, tok + half)
             if half == 1:
-                put_units(2 * f, 2)
-            tick(2 * f - 1 + half)
+                @pl.when(tok + 2 == per)
+                def _():
+                    put_unit(2 * f)
+                    put_unit(2 * f + 1)
+            rolling_tick(i, half)
         return carry
 
-    lax.fori_loop(0, turns, feed_one, 0)
+    lax.fori_loop(0, feeds * per // 2, feed_pair, 0)
+    clock[0] = feeds * per - early
+    flying.update({u: 2 * u for u in range(2 * feeds) if 2 * u < clock[0]})
+    waiting.extend(u for u in range(2 * feeds) if 2 * u >= clock[0])
 
     def stage_copy(buffer, target, b):
         slot = lax.rem(b, 2)
         return pltpu.make_async_copy(buffer.at[slot], target.at[:, pl.ds(pl.multiple_of(b * block, block), block), :], stage_sems.at[slot])
 
-    def finish_two(b, carry):
-        norm_sum, cot_sum = carry
+    def finish_two(b, norm_sum, cot_sum):
         at = at_block(b)
 
         @pl.when(b >= 2)
@@ -717,13 +761,12 @@
         return norm_sum, cot_sum
 
     zero = jnp.zeros((8, width), F32)
-    norm_sum, cot_sum = lax.fori_loop(0, blocks, finish_two, (zero, zero))
+    norm_sum, cot_sum = beat(blocks, finish_two, 2, zero, zero)
     for b in (blocks - 2, blocks - 1):
         stage_copy(mixed_s, mixed_out, b).wait()
     put_small(20, jnp.sum(norm_sum, axis=0, keepdims=True))
     put_small(24, sums_v[0:1])
     put_small(40, jnp.sum(cot_sum, axis=0, keepdims=True))
-    tick(2 * turns - 1)
 
     loads[4].wait()
     loads[5].wait()
@@ -733,13 +776,14 @@
         lanes = pl.ds(j * wide, wide)
         return pltpu.make_async_copy(source.at[at_block(b), lanes], buffer.at[slot], stream_sems.at[k, slot])
 
-    flows = [mixed_v, flow_v]
+    def half_of(refs, j):
+        return refs[j // 2], slice(UNIT * (j % 2), UNIT * (j % 2) + UNIT)
 
     def first_pass(j):
+        flows, lanes = half_of((mixed_v, middle_v), j)
         stream(decay_s, decay_in, j, blocks - 1, 0).start()
 
-        def one(i, carry):
-            product, flow = carry
+        def one(i, product, flow):
             b = blocks - 1 - i
             at = at_block(b)
 
@@ -747,7 +791,7 @@
             def _():
                 stream(decay_s, decay_in, j, b - 1, 0).start()
             back = dot_nt(low_v[at], w_out_v[pl.ds(j * wide, wide)])
-            flows[j][at] = back
+            flows[at, lanes] = back
             stream(decay_s, decay_in, j, b, 0).wait()
             slot = lax.rem(b, 2)
             for t in reversed(range(block)):
@@ -757,60 +801,60 @@
                 product = decay * product
             return product, flow
 
-        product, flow = lax.fori_loop(0, blocks, one, (jnp.ones((rows, wide), F32), jnp.zeros((rows, wide), F32)))
+        product, flow = lax.fori_loop(0, blocks, lambda i, c: one(i, *c), (jnp.ones((rows, wide), F32), jnp.zeros((rows, wide), F32)))
+        tick()
         chain.start(j, product, flow)
 
-    def grad_out(j):
-        slot = (2 * turns + j) % slots
-
-        def one(tok, carry):
-            at = at_block(tok, big)
-            part = dot_tn(state_v[at, pl.ds(j * UNIT, UNIT)], low_v[at])
-
-            @pl.when(tok == 0)
-            def _():
-                grads[slot] = part
-
-            @pl.when(tok > 0)
-            def _():
-                grads[slot] = grads[slot] + part
-            return carry
-
-        lax.fori_loop(0, per, one, 0)
-        put_units(2 * turns + j, 1)
-
-    now = 2 * turns
-    for j in range(halves):
-        first_pass(j)
-        grad_out(j)
-        for i in range(j):
-            if j - 1 - i < chain.rounds:
-                chain.advance(i, j - 1 - i)
-        tick(now)
-        now += 1
-
-    loads[7].wait()
+    def grad_out():
+        for j in range(hidden // SPAN):
+            def one(tok, carry):
+                at = at_block(tok, big)
+                gather(2 * feeds + j, 0, dot_tn(state_v[at, pl.ds(j * SPAN, SPAN)], low_v[at]), tok == 0)
+                return carry
+
+            lax.fori_loop(0, per, one, 0)
+            put_unit(2 * feeds + j)
+            waiting.append(2 * feeds + j)
+            tick()
+
     gains_one = gain_one[...]
 
-    def norm_one(b, carry):
+    def norm_one(b):
         at = at_block(b)
         value = x_v[at].astype(F32)
         scale = lax.rsqrt(jnp.mean(value * value, axis=-1, keepdims=True) + EPS)
         turned_v[:, at] = jnp.swapaxes(value * scale * gains_one, 0, 1).astype(BF16)
-        middle_v[at] = jnp.zeros_like(value)
-        return carry
+        return ()
+
+    work = [functools.partial(first_pass, j) for j in range(parts)]
+    work += [grad_out]
+
+    def turn():
+        loads[7].wait()
+        beat(blocks, norm_one, 1)
+
+    work.append(turn)
+    for step in range(max(len(work), parts + chain.rounds)):
+        if step < len(work):
+            work[step]()
+        else:
+            tick()
+        for i in range(parts):
+            if 0 <= step - 1 - i < chain.rounds:
+                chain.advance(i, step - 1 - i)
 
     streams = ((decay_s, decay_in), (fade_s, fade_in), (rise_s, rise_in), (weight_s, weight_in), (lean_s, lean_in))
-    backs = [lambda at: (state_v, (at, slice(0, UNIT))), lambda at: (state_v, (at, slice(UNIT, 2 * UNIT))), lambda at: (cot_v, (at, slice(None)))]
+    cand_refs = (low_v, cand_v)
+    input_refs = (cot_v, w_down_v)
 
     def second_pass(j):
+        flows, lanes = half_of((mixed_v, middle_v), j)
+        to_input, to_cand = half_of(input_refs, j)[0], half_of(cand_refs, j)[0]
         for k, (buffer, source) in enumerate(streams):
             stream(buffer, source, j, blocks - 1, k).start()
 
-        def one(i, carry):
-            flow, sum_f, sum_i = carry
+        def one(i, flow, sum_f, sum_i):
             b = blocks - 1 - i
-            at = at_block(b)
             slot = lax.rem(b, 2)
 
             @pl.when(b > 0)
@@ -819,67 +863,48 @@
                     stream(buffer, source, j, b - 1, k).start()
             for k, (buffer, source) in enumerate(streams):
                 stream(buffer, source, j, b, k).wait()
-            parts = []
             for t in reversed(range(block)):
                 here = slice(t * rows, (t + 1) * rows)
                 there = pl.ds(pl.multiple_of(b * size + t * rows, rows), rows)
-                reach = flows[j][there] + flow
+                reach = flows[there, lanes] + flow
                 flow = decay_s[slot, here] * reach
                 lean = reach * lean_s[slot, here].astype(F32)
                 grad_f = fade_s[slot, here].astype(F32) * lean
                 grad_i = -(rise_s[slot, here].astype(F32) * lean)
                 sum_f, sum_i = sum_f + grad_f, sum_i + grad_i
-                state_v[there, 0:UNIT] = grad_f.astype(BF16)
-                state_v[there, UNIT : 2 * UNIT] = grad_i.astype(BF16)
-                cot_v[there] = (weight_s[slot, here].astype(F32) * reach).astype(BF16)
+                state_v[there, wide * j : wide * j + wide] = grad_f.astype(BF16)
+                to_input[there, lanes] = grad_i.astype(BF16)
+                to_cand[there, lanes] = (weight_s[slot, here].astype(F32) * reach).astype(BF16)
             return flow, sum_f, sum_i
 
         none = jnp.zeros((rows, wide), F32)
-        unused, sum_f, sum_i = lax.fori_loop(0, blocks, one, (join[j, 1], none, none))
-        put_small(4 + 4 * j, jnp.sum(sum_f, axis=0, keepdims=True))
-        put_small(12 + 4 * j, jnp.sum(sum_i, axis=0, keepdims=True))
-
-    def project(j, k, base):
-        slot = (base + k) % slots
+        unused, sum_f, sum_i = beat(blocks, one, 2, join[j, 1], none, none)
+        put_small(4 + 2 * j, jnp.sum(sum_f, axis=0, keepdims=True))
+        put_small(12 + 2 * j, jnp.sum(sum_i, axis=0, keepdims=True))
+
+    def grad_in(j):
+        unit = 2 * feeds + hidden // SPAN + 3 * j
 
         def one(tok, carry):
             at = at_block(tok, big)
-            ref, index = backs[k](at)
-            piece = ref[index]
-            part = dot(turned_v[:, at], piece)
-            columns = pl.ds(k * hidden + j * wide, wide)
-            middle_v[at] = middle_v[at] + dot_nt(piece, w_in_v[:, columns])
-
-            @pl.when(tok == 0)
-            def _():
-                grads[slot] = part
-
-            @pl.when(tok > 0)
-            def _():
-                grads[slot] = grads[slot] + part
+            turned = turned_v[:, at]
+            lanes = half_of(input_refs, j)[1]
+            pieces = (state_v[at, wide * j : wide * j + wide], half_of(input_refs, j)[0][at, lanes], half_of(cand_refs, j)[0][at, lanes])
+            for k, piece in enumerate(pieces):
+                gather(*plan[unit + k][:2], dot(turned, piece), tok == 0)
             return carry
 
         lax.fori_loop(0, per, one, 0)
-        put_units(base + k, 1)
-
-    base = 2 * turns + halves
-    lax.fori_loop(0, blocks, norm_one, 0)
-    for step in range(halves, halves + chain.rounds):
-        for i in range(halves):
-            if 0 <= step - 1 - i < chain.rounds:
-                chain.advance(i, step - 1 - i)
-    tick(now)
-    now += 1
+        for k in range(3):
+            put_unit(unit + k)
+            waiting.append(unit + k)
+        tick()
+
+    for j in range(parts):
+        second_pass(j)
+        grad_in(j)
+
     loads[6].wait()
-    for j in range(halves):
-        second_pass(j)
-        tick(now)
-        now += 1
-        for k in range(3):
-            project(j, k, base + 3 * j)
-            if k < 2 or j == 0:
-                tick(now)
-                now += 1
 
     def finish_one(b, norm_sum):
         at = at_block(b)
@@ -887,7 +912,12 @@
         @pl.when(b >= 2)
         def _():
             stage_copy(tokens_s, tokens_out, b - 2).wait()
-        value, grad = x_v[at].astype(F32), middle_v[at]
+        grad = dot_nt(state_v[at], w_in_v[:, :hidden])
+        for k, refs in enumerate((input_refs, cand_refs)):
+            for half in range(2):
+                columns = pl.ds((k + 1) * hidden + half * SPAN, SPAN)
+                grad = grad + dot_nt(refs[half][at], w_in_v[:, columns])
+        value = x_v[at].astype(F32)
         scale = lax.rsqrt(jnp.mean(value * value, axis=-1, keepdims=True) + EPS)
         plain = value * scale
         norm_sum = norm_sum + jnp.sum((grad * plain).reshape(size // 8, 8, width), axis=0)
@@ -895,23 +925,25 @@
         back = second_v[at] + scale * (lean - plain * jnp.mean(lean * plain, axis=-1, keepdims=True))
         tokens_s[lax.rem(b, 2)] = jnp.swapaxes(back.reshape(block, rows, width), 0, 1)
         stage_copy(tokens_s, tokens_out, b).start()
-        return norm_sum
-
-    norm_sum = lax.fori_loop(0, blocks, finish_one, jnp.zeros((8, width), F32))
+        return (norm_sum,)
+
+    (norm_sum,) = beat(blocks, finish_one, 8, jnp.zeros((8, width), F32))
     put_small(0, jnp.sum(norm_sum, axis=0, keepdims=True))
     if ringed:
-        def drain(t, carry):
-            tick(t)
-            return carry
-
-        lax.fori_loop(now, units + len(holes) + STAGES, drain, 0)
+        step = 0
+        while step <= DOUBLINGS or waiting or any(clock[0] <= flying[unit] + pace(unit)[-1] for unit in flying):
+            tick()
+            if step <= DOUBLINGS:
+                small.step(step)
+            step += 1
+        copy = pltpu.make_async_copy(own_v.at[DOUBLINGS], small_out.at[0], load_sems.at[0])
     else:
         copy = pltpu.make_async_copy(small_v, small_out.at[0], load_sems.at[0])
-        copy.start()
-        copy.wait()
+    copy.start()
+    copy.wait()
     for b in (blocks - 2, blocks - 1):
         stage_copy(tokens_s, tokens_out, b).wait()
-    for j in range(halves):
+    for j in range(parts):
         chain.finish(j)
 
 
@@ -924,35 +956,40 @@
     block = 16
     size = block * rows
     wide = UNIT
-    halves = hidden // wide
-    units = 2 * (inner // UNIT) + halves + 3 * halves
-    slots = 10
-    first = 2 * (inner // UNIT) + halves
-    holes = (first, first + 1, first + 5)
+    parts = hidden // wide
+    feeds = inner // SPAN
+    whole = 2 * feeds + hidden // SPAN
+    plan = [(u, 0, WIDE) for u in range(whole)]
+    for j in range(parts):
+        slot = (whole + 2 * j) % SLOTS
+        plan += [(slot, 0, UNIT), (slot, UNIT, UNIT), (slot + 1, 0, UNIT)]
+    units = len(plan)
     anywhere = pl.BlockSpec(memory_space=pl.ANY)
     vmem = pl.BlockSpec(memory_space=pltpu.VMEM)
     shape = jax.ShapeDtypeStruct
     if ringed:
-        more = sum_scratch(units, slots, UNIT, width) + sum_scratch(1, 1, SMALL_ROWS, 128)
+        first, *others = sum_scratch(units, SLOTS)
+        more = [first, pltpu.VMEM((DOUBLINGS + 1, SMALL_ROWS, 128), F32), *others]
+        more += [pltpu.VMEM((DOUBLINGS, SMALL_ROWS, 128), F32)] + [pltpu.SemaphoreType.DMA((DOUBLINGS,))] * 2
     else:
-        more = [pltpu.VMEM((slots, UNIT, width), F32), pltpu.VMEM((1, SMALL_ROWS, 128), F32)]
+        more = [pltpu.VMEM((SLOTS, SPAN, WIDE), F32), pltpu.VMEM((1, SMALL_ROWS, 128), F32)]
     return pl.pallas_call(
-        functools.partial(back_kernel, ringed, count, rows, steps, units, slots, holes, block),
+        functools.partial(back_kernel, ringed, count, rows, steps, plan, block),
         out_shape=(
-            shape(shape_in, BF16), shape(shape_in, F32), shape((units, UNIT, width), F32), shape((1, SMALL_ROWS, 128), F32),
+            shape(shape_in, BF16), shape(shape_in, F32), shape((units, SPAN, WIDE), F32), shape((1, SMALL_ROWS, 128), F32),
         ),
         in_specs=[anywhere] * 9 + [vmem] * 4 + [anywhere] * 4,
         out_specs=(anywhere,) * 4,
         scratch_shapes=[
-            pltpu.VMEM((total, width), F32), pltpu.VMEM((total, width), F32), pltpu.VMEM((total, width), F32), pltpu.VMEM((total, width), F32),
+            pltpu.VMEM((total, width), F32), pltpu.VMEM((total, width), F32), pltpu.VMEM((total, width), F32),
             pltpu.VMEM((total, hidden), BF16), pltpu.VMEM((total, width), BF16), pltpu.VMEM((total, width), BF16), pltpu.VMEM((total, width), BF16),
-            pltpu.VMEM((width, total), BF16),
+            pltpu.VMEM((total, width), BF16), pltpu.VMEM((width, total), BF16),
             pltpu.VMEM(w_in.shape, BF16), pltpu.VMEM(w_out.shape, BF16), pltpu.VMEM(w_up.shape, BF16), pltpu.VMEM(w_down.shape, BF16),
             pltpu.VMEM((2, size, wide), F32), pltpu.VMEM((2, size, wide), BF16), pltpu.VMEM((2, size, wide), BF16),
             pltpu.VMEM((2, size, wide), BF16), pltpu.VMEM((2, size, wide), BF16),
             pltpu.VMEM((2, rows, block, width), BF16), pltpu.VMEM((2, rows, block, width), F32), pltpu.VMEM((8, inner), F32),
             pltpu.SemaphoreType.DMA((8,)), pltpu.SemaphoreType.DMA((5, 2)), pltpu.SemaphoreType.DMA((2,)),
-            *chain_scratch(halves, count, rows, wide),
+            *chain_scratch(parts, count, rows, wide),
             *more,
         ],
         compiler_params=pltpu.CompilerParams(collective_id=cid, has_side_effects=True, vmem_limit_bytes=63 * 2**20),
@@ -961,9 +998,65 @@
     )(x, cot, middle, state, decay, fade, rise, weight, lean, gain_one.reshape(1, -1), gain_two.reshape(1, -1), up_bias.reshape(1, -1), down_bias.reshape(1, -1), w_in, w_out, w_up, w_down)
 
 
+def settle_kernel(places, mixed, tokens, units, small, *refs):
+    outs, (mixed_v, tokens_v, units_v, reads, writes) = refs[:-5], refs[-5:]
+    copies = []
+    for k in range(mixed.shape[0] // 4):
+        some = pl.ds(4 * k, 4)
+        copies.append((tokens.at[some], tokens_v.at[some], outs[1].at[some]))
+        copies.append((mixed.at[some], mixed_v.at[some], outs[0].at[some]))
+    for u, length, array, row, column in places:
+        lanes = pl.ds(0, length)
+        copies.append((units.at[u, :, lanes], units_v.at[u, :, lanes], outs[2 + array].at[pl.ds(row, SPAN), pl.ds(column, length)]))
+    moves = [
+        (pltpu.make_async_copy(a, b, reads.at[k]), pltpu.make_async_copy(b, c, writes.at[k])) for k, (a, b, c) in enumerate(copies)
+    ]
+    for read, write in moves:
+        read.start()
+    row = 0
+    for out in outs[6:]:
+        out[...] = small[0, pl.ds(row, out.shape[0])]
+        row += out.shape[0]
+    for read, write in moves:
+        read.wait()
+        write.start()
+    for read, write in moves:
+        write.wait()
+
+
+def settle(mixed, tokens, units, small, hidden, inner):
+    width = tokens.shape[-1]
+    parts = hidden // UNIT
+    feeds = inner // SPAN
+    places = []
+    for f in range(feeds):
+        places += [(2 * f, SPAN, 3, f * SPAN, 0), (2 * f + 1, SPAN, 2, 0, f * SPAN)]
+    places += [(2 * feeds + j, SPAN, 1, j * SPAN, 0) for j in range(hidden // SPAN)]
+    for j in range(parts):
+        places += [(len(places) + k, UNIT, 0, 0, k * hidden + j * UNIT) for k in range(3)]
+    anywhere = pl.BlockSpec(memory_space=pl.ANY)
+    vmem = pl.BlockSpec(memory_space=pltpu.VMEM)
+    shape = jax.ShapeDtypeStruct
+    lengths = (width, hidden, hidden, width, inner, width)
+    return pl.pallas_call(
+        functools.partial(settle_kernel, places),
+        out_shape=(
+            shape(mixed.shape, mixed.dtype), shape(tokens.shape, F32), shape((width, 3 * hidden), F32), shape((hidden, width), F32),
+            shape((width, inner), F32), shape((inner, width), F32), *(shape((n // 128, 128), F32) for n in lengths),
+        ),
+        in_specs=[anywhere] * 3 + [vmem],
+        out_specs=(anywhere,) * 6 + (vmem,) * 6,
+        scratch_shapes=[
+            pltpu.VMEM(mixed.shape, mixed.dtype), pltpu.VMEM(tokens.shape, F32), pltpu.VMEM(units.shape, F32),
+            pltpu.SemaphoreType.DMA((mixed.shape[0] // 2 + len(places),)), pltpu.SemaphoreType.DMA((mixed.shape[0] // 2 + len(places),)),
+        ],
+        compiler_params=pltpu.CompilerParams(vmem_limit_bytes=48 * 2**20),
+        name="settle",
+    )(mixed, tokens, units, small)
+
+
 def on_device(tokens, cotangent, reset_pos, norm1_gain, w_in, forget_bias, input_bias, w_out, norm2_gain, w_up, up_bias, w_down, down_bias):
     ringed = lax.axis_size("seq") == 8 and lax.axis_size("rows") == 4
-    width = tokens.shape[-1]
     hidden, inner = w_out.shape[0], w_down.shape[0]
     kept = front(tokens, cotangent, reset_pos, norm1_gain, w_in, forget_bias, input_bias, w_out)
     mixed, grad_tokens, units, small = back(
@@ -971,22 +1064,9 @@
     )
     if not ringed:
         units, small = lax.psum((units, small), ("seq", "rows"))
-    feeds = inner // UNIT
-    halves = hidden // UNIT
-    grad_down = jnp.concatenate([units[2 * f] for f in range(feeds)], axis=0)
-    grad_up = jnp.concatenate([units[2 * f + 1] for f in range(feeds)], axis=1)
-    grad_out = units[2 * feeds : 2 * feeds + halves].reshape(hidden, width)
-    base = 2 * feeds + halves
-    grad_in = jnp.concatenate([units[base + 3 * j + k] for k in range(3) for j in range(halves)], axis=1)
-    flat = small[0]
-
-    def rows_of(first, length):
-        return flat[first : first + length // 128].reshape(length)
-
-    return (
-        mixed, grad_tokens, rows_of(0, width), grad_in, rows_of(4, hidden), rows_of(12, hidden), grad_out,
-        rows_of(20, width), grad_up, rows_of(24, inner), grad_down, rows_of(40, width),
-    )
+    mixed, grad_tokens, grad_in, grad_out, grad_up, grad_down, *rest = settle(mixed, grad_tokens, units, small, hidden, inner)
+    norm_one, forget, inputs, norm_two, up, down = (one.reshape(-1) for one in rest)
+    return mixed, grad_tokens, norm_one, grad_in, forget, inputs, grad_out, norm_two, grad_up, up, grad_down, down
 
 
 def solution(mesh):

time: 292 us -> 271 us (0.928)
  local copies, waits for them, and re-layouts: 31.1 us -> 3.68 us
  Pallas kernels: 253 us -> 266 us
  other arithmetic: 6.8 us -> 0 us
    pallas_call x0 -> x1, Pallas kernels: none -> 16.3 us  [settle(): pl.pallas_call(functools.partial(settle_kernel, places), out_shape=(shape...]
    unnamed x14 -> x5, local copies, waits for them, and re-layouts: 19 us -> 3.68 us
    concatenate x2 -> x0, other arithmetic: 6.8 us -> none  [the longest x1 4.41 us: on_device(): grad_down = jnp.concatenate([units[2 * f] for f in range(feeds)], axis=0)]
    reshape x3 -> x0, local copies, waits for them, and re-layouts: 3.94 us -> none  [rows_of(): return flat[first:first + length // 128].reshape(length)]
    pallas_call x1, Pallas kernels: 217 us -> 214 us  [back(): pl.pallas_call(functools.partial(back_kernel, ringed, count, rows, steps,...]
    slice x1 -> x0, local copies, waits for them, and re-layouts: 3.24 us -> none  [on_device(): grad_out = units[2 * feeds:2 * feeds + halves].reshape(hidden, width)]
where the time goes in v3:
time: 271 us; the launch traced here: 270 us
  Pallas kernels  266 us (98%)
  local copies, waits for them, and re-layouts  3.68 us (1%)
    pallas_call x1, Pallas kernels, back(): pl.pallas_call(functools.partial(back_kernel, ringed, count, rows, steps,...  214 us
    pallas_call x1, Pallas kernels, front(): pl.pallas_call(functools.partial(front_kernel, count, rows, steps, chunk,...  35.4 us
    pallas_call x1, Pallas kernels, settle(): pl.pallas_call(functools.partial(settle_kernel, places), out_shape=(shape...  16.3 us

profile of v3, /device:TPU:0, one launch (start us, length us, event | category | flops | bytes accessed | tf_op | source)
XLA Modules:
  0.0 270.2 jit_solution(6353923740333789915)
XLA Ops:
  0.6 1.4 copy.25.reset
  2.0 35.4 %front.1 = (bf16[2048,512]{1,0:T(8,128)(2,1)}, bf16[2048,512]{1,0:T(8,128)(2,1)}, f32[2048,512]{1,0:T(8,128)}, bf16[2048,1024]{1,0:T(8,128)(2,1)}, f32[2048,1024...) custom-call(bf16[16,128,512]{2,1,0:T(8,128)(2,1)} %tokens.1, ...), custom_call_target="tpu_custom_call" | custom-call | flops 8589934592 | bytes 41943040 | tf_op jit(solution)/shard_map/front/pallas_call | solution.py:319
  37.4 214.0 %back.1 = (bf16[16,128,512]{2,1,0:T(8,128)(2,1)}, f32[16,128,512]{2,1,0:T(8,128)}, f32[22,512,512]{2,1,0:T(8,128)}, f32[1,48,128]{2,1,0:T(8,128)}) custom-call(bf16[2048,512]{1,0:T(8,128)(2,1)} %get-tuple-element.37.x_in, bf16[2048,512]{1,0:T(8,128)(2,1)} %get-tuple-element.38.cot_in, f32[2048,512]{1,0:T(8,128)} %get-tuple-element.39.middle_in, ...), custom_call_target="tpu_custom_call" | custom-call | flops 42949672960 | bytes 83886080 | tf_op jit(solution)/shard_map/back/pallas_call | solution.py:976
  251.4 0.0 copy-start
  251.4 1.6 copy-done
  253.0 0.0 copy-start.1
  253.0 0.7 copy-done.1
  253.7 16.3 %settle.1 = (bf16[16,128,512]{2,1,0:T(8,128)(2,1)}, f32[16,128,512]{2,1,0:T(8,128)}, f32[512,3072]{1,0:T(8,128)}, f32[1024,512]{1,0:T(8,128)}, f32[512,2048]{1,0...) custom-call(bf16[16,128,512]{2,1,0:T(8,128)(2,1)S(1)} %copy-done, ...), custom_call_target="tpu_custom_call" | custom-call | tf_op jit(solution)/shard_map/settle/pallas_call | solution.py:1041
Async XLA Ops:
  251.4 1.6 copy-start
  253.0 0.7 copy-start.1

commit v4 on v3

--- a/solution.py
+++ b/solution.py
@@ -16,11 +16,12 @@
 SPAN = 512
 UNIT = 256
 WIDE = 512
-SLOTS = 12
+SLOTS = 10
+SIDE = 2
 SMALL_ROWS = 48
 DOUBLINGS = 5
 SLOW = (0, 1, 3, 6, 8, 10, 11, 12, 14, 16, 19, 21, 22)
-FAST = (0, 1, 3, 5, 7, 8, 9, 10, 11, 13, 15, 17, 18)
+FAST = (0, 1, 4, 8, 11, 13, 15, 17, 19, 22, 26, 29, 30)
 
 
 def place():
@@ -185,10 +186,7 @@
         lanes = pl.ds(j * chunk, chunk)
         shift_f, shift_i = -forget_bias[:, lanes], -input_bias[:, lanes]
 
-        def one(b, carry):
-            product, end = carry
-            at = pl.ds(pl.multiple_of(b * size, size), size)
-            project = dot(normed_v[at], w_v[j])
+        def some(project, at, product, end):
             neg_f = shift_f - project[:, :chunk]
             neg_i = shift_i - project[:, chunk : 2 * chunk]
             cand = project[:, 2 * chunk :]
@@ -204,8 +202,7 @@
             cand_v[at, lanes] = cand
             update = weight * cand
             update_v[at, lanes] = update
-            keep = jnp.concatenate([keep_v[at]] * (chunk // 128), axis=1)
-            decay = decay * keep
+            decay = decay * jnp.concatenate([keep_v[at]] * (chunk // 128), axis=1)
             decay_v[at, lanes] = decay
             for t in range(block):
                 here = decay[t * rows : (t + 1) * rows]
@@ -213,31 +210,35 @@
                 product = here * product
             return product, end
 
+        def one(b, carry):
+            places = [pl.ds(pl.multiple_of((b * SIDE + k) * size, size), size) for k in range(SIDE)]
+            for at in places:
+                carry = some(dot(normed_v[at], w_v[j]), at, *carry)
+            return carry
+
         start = (jnp.ones((rows, chunk), F32), jnp.zeros((rows, chunk), F32))
-        return lax.fori_loop(0, blocks, one, start)
+        return lax.fori_loop(0, blocks // SIDE, one, start)
 
     def scan(j):
         lanes = pl.ds(j * chunk, chunk)
 
         def one(b, state):
-            at = pl.ds(pl.multiple_of(b * size, size), size)
-            states = []
             for t in range(block):
                 here = pl.ds(pl.multiple_of(b * size + t * rows, rows), rows)
                 keep = jnp.concatenate([keep_v[here]] * (chunk // 128), axis=1)
                 lean_v[j % 2, here] = (keep * state - cand_v[here, lanes]).astype(BF16)
                 state = decay_v[here, lanes] * state + update_v[here, lanes]
-                states.append(state.astype(BF16))
-            low = jnp.concatenate(states, axis=0)
-            state_v[at, lanes] = low
-            add = dot(low, w_out_v[lanes])
-            if j == 0:
-                middle_v[at] = x_v[at].astype(F32) + add
-            else:
-                middle_v[at] = middle_v[at] + add
+                state_v[here, lanes] = state.astype(BF16)
             return state
 
         lax.fori_loop(0, blocks, one, join[j, 1])
+
+    def project_out(b, carry):
+        at = pl.ds(pl.multiple_of(b * 2 * size, 2 * size), 2 * size)
+        middle_v[at] = x_v[at].astype(F32) + dot(state_v[at], w_out_v[...])
+        copy = pltpu.make_async_copy(middle_v.at[at], middle_out.at[at], out_sems.at[2 + 6 * parts])
+        copy.start()
+        return carry
 
     def put(source, target, slot, wait=False):
         copy = pltpu.make_async_copy(source, target, out_sems.at[slot])
@@ -295,7 +296,7 @@
             scan_outs(ready)
             ready += 1
         step += 1
-    put(middle_v, middle_out, 2 + 6 * parts)
+    lax.fori_loop(0, blocks // 2, project_out, 0)
     for j in range(parts):
         if j >= parts - 2:
             gate_outs(j, True)
@@ -341,10 +342,11 @@
 
 
 class Summing:
-    def __init__(self, plan, grads, half_in, part_in, up_in, down_in, last_in, send, recv, local, result):
+    def __init__(self, plan, grads, half_in, part_in, lines_in, last_in, send, recv, local, free, result):
         self.plan, self.grads = plan, grads
-        self.half_in, self.part_in, self.up_in, self.down_in, self.last_in = half_in, part_in, up_in, down_in, last_in
-        self.result, self.send, self.recv, self.local = result, send, recv, local
+        self.whole = sum(width == WIDE for slot, column, width in plan)
+        self.half_in, self.part_in, self.lines_in, self.last_in = half_in, part_in, lines_in, last_in
+        self.result, self.send, self.recv, self.local, self.free = result, send, recv, local, free
         x, y, z, core = place()
         self.z = z
         first = core == 0
@@ -380,25 +382,71 @@
     def done(self, u, start, count):
         return self.result.at[u, pl.ds(pl.multiple_of(start, 8), count), pl.ds(0, self.slot_of(u)[2])]
 
-    def land(self, ref, u, slots, start, count):
-        return ref.at[lax.rem(u, slots), pl.ds(start, count), pl.ds(0, self.slot_of(u)[2])]
+    def land(self, ref, wide, u, start, count):
+        if self.slot_of(u)[2] == WIDE:
+            return ref.at[lax.rem(u, wide), pl.ds(start, count)]
+        turn = (u - self.whole) % (2 * (ref.shape[0] - wide))
+        return ref.at[wide + turn // 2, pl.ds(start, count), pl.ds(turn % 2 * UNIT, UNIT)]
+
+    def turns(self, kind, u):
+        ref, wide = ((self.half_in, 2), (self.part_in, 3), (self.lines_in, 3), (self.lines_in, 3))[kind]
+        if self.slot_of(u)[2] == WIDE:
+            return wide, 0, self.whole
+        return 2 * (ref.shape[0] - wide), self.whole, len(self.plan)
+
+    def claim(self, kind, u):
+        apart, first, last = self.turns(kind, u)
+        if isinstance(u, int):
+            if u - apart >= first:
+                pl.semaphore_wait(self.free.at[kind, u - apart], 1)
+        else:
+            @pl.when(u >= apart)
+            def _():
+                pl.semaphore_wait(self.free.at[kind, u - apart], 1)
+
+    def release(self, kind, u, sender):
+        apart, first, last = self.turns(kind, u)
+
+        def signal():
+            pl.semaphore_signal(self.free.at[kind, u], inc=1, device_id=sender, device_id_type=MESH)
+
+        if isinstance(u, int):
+            if u + apart < last:
+                signal()
+        else:
+            pl.when(u + apart < last)(signal)
+
+    def land_half(self, u):
+        return self.land(self.half_in, 2, u, 0, self.n_half)
+
+    def land_part(self, u):
+        return self.land(self.part_in, 3, u, 0, self.n_part)
+
+    def land_up(self, u, z):
+        return self.land(self.lines_in, 3, u, 0, self.n_line * (4 - z))
+
+    def land_down(self, u, z):
+        return self.land(self.lines_in, 3, u, self.n_line * (4 - z) if z > 0 else 0, self.n_line * (z + 1))
+
+    def land_last(self, u):
+        return self.land(self.last_in, self.whole, u, 0, self.n_tip)
 
     def c_half(self, u):
-        return self.copy(0, u, self.rows(u, self.other_half, self.n_half), self.land(self.half_in, u, 4, 0, self.n_half), self.sibling)
+        return self.copy(0, u, self.rows(u, self.other_half, self.n_half), self.land_half(u), self.sibling)
 
     def c_part(self, u):
-        return self.copy(1, u, self.rows(u, self.other_part, self.n_part), self.land(self.part_in, u, 4, 0, self.n_part), self.near)
+        return self.copy(1, u, self.rows(u, self.other_part, self.n_part), self.land_part(u), self.near)
 
     def c_up(self, u, z):
         low, rest = self.n_line * (z + 1), self.n_line * (3 - z)
-        return self.copy(2, u, self.rows(u, self.part + low, rest), self.land(self.up_in, u, 8, low - self.n_line, rest), self.above)
+        return self.copy(2, u, self.rows(u, self.part + low, rest), self.land_up(u, z + 1), self.above)
 
     def c_down(self, u, z):
         rest = self.n_line * z
-        return self.copy(3, u, self.rows(u, self.part, rest), self.land(self.down_in, u, 8, 0, rest), self.below)
+        return self.copy(3, u, self.rows(u, self.part, rest), self.land_down(u, z - 1), self.below)
 
     def c_last(self, u):
-        return self.copy(4, u, self.rows(u, self.other_tip, self.n_tip), self.last_in.at[u, :, pl.ds(0, self.slot_of(u)[2])], self.far)
+        return self.copy(4, u, self.rows(u, self.other_tip, self.n_tip), self.land_last(u), self.far)
 
     def c_own(self, u):
         return pltpu.make_async_copy(self.rows(u, self.tip, self.n_tip), self.done(u, self.tip, self.n_tip), self.local.at[u])
@@ -424,7 +472,7 @@
 
     def add(self, u, start, count, ref):
         slot, column, width = self.slot_of(u)
-        step = math.gcd(count, 64)
+        step = min(count, 128)
         lanes = pl.ds(column, width)
 
         def one(i, carry):
@@ -433,7 +481,30 @@
             self.grads[slot, here, lanes] = self.grads[slot, here, lanes] + ref[there]
             return carry
 
-        lax.fori_loop(0, count // step, one, 0)
+        if count == step:
+            one(0, 0)
+        else:
+            lax.fori_loop(0, count // step, one, 0)
+
+    def settle_sums(self, units):
+        def sent(k):
+            for u in units:
+                if k < 3:
+                    self.c_up(u, k).wait_send()
+                if k > 0:
+                    self.c_down(u, k).wait_send()
+
+        self.at_each(sent)
+
+    def settle_lines(self, units):
+        def sent(k):
+            for u in units:
+                if k < 3:
+                    self.c_rise(u, k).wait_send()
+                if k > 0:
+                    self.c_fall(u, k).wait_send()
+
+        self.at_each(sent)
 
     def at_each(self, action):
         for k in range(4):
@@ -442,14 +513,18 @@
     def stage(self, s, u):
         z = self.z
         if s == 0:
+            self.claim(0, u)
             self.c_half(u).start()
         elif s == 1:
             self.c_half(u).wait()
-            self.add(u, self.half, self.n_half, self.land(self.half_in, u, 4, 0, self.n_half))
+            self.add(u, self.half, self.n_half, self.land_half(u))
+            self.release(0, u, self.sibling)
+            self.claim(1, u)
             self.c_part(u).start()
         elif s == 2:
             self.c_part(u).wait()
-            self.add(u, self.part, self.n_part, self.land(self.part_in, u, 4, 0, self.n_part))
+            self.add(u, self.part, self.n_part, self.land_part(u))
+            self.release(1, u, self.near)
         if 2 <= s <= 5:
             up, down = s - 2, 5 - s
 
@@ -458,8 +533,10 @@
                 if up > 0:
                     self.c_up(u, up - 1).wait_recv()
                     low, rest = self.n_line * up, self.n_line * (4 - up)
-                    self.add(u, self.part + low, rest, self.land(self.up_in, u, 8, low - self.n_line, rest))
+                    self.add(u, self.part + low, rest, self.land_up(u, up))
+                    self.release(2, u, self.below)
                 if up < 3:
+                    self.claim(2, u)
                     self.c_up(u, up).start()
 
             @pl.when(z == down)
@@ -467,21 +544,16 @@
                 if down < 3:
                     self.c_down(u, down + 1).wait_recv()
                     rest = self.n_line * (down + 1)
-                    self.add(u, self.part, rest, self.land(self.down_in, u, 8, 0, rest))
+                    self.add(u, self.part, rest, self.land_down(u, down))
+                    self.release(3, u, self.above)
                 if down > 0:
+                    self.claim(3, u)
                     self.c_down(u, down).start()
         if s == 5:
             self.c_last(u).start()
         elif s == 6:
-            def sent(k):
-                if k < 3:
-                    self.c_up(u, k).wait_send()
-                if k > 0:
-                    self.c_down(u, k).wait_send()
-
-            self.at_each(sent)
             self.c_last(u).wait()
-            self.add(u, self.tip, self.n_tip, self.last_in.at[u, :, pl.ds(0, self.slot_of(u)[2])])
+            self.add(u, self.tip, self.n_tip, self.land_last(u))
             self.c_far(u, self.tip).start()
             self.c_own(u).start()
         elif s == 7:
@@ -507,13 +579,6 @@
         if s == 10:
             self.c_near(u, self.part).start()
         elif s == 11:
-            def sent(k):
-                if k < 3:
-                    self.c_rise(u, k).wait_send()
-                if k > 0:
-                    self.c_fall(u, k).wait_send()
-
-            self.at_each(sent)
             self.c_near(u, self.part).wait_send()
             self.c_near(u, self.other_part).wait_recv()
             self.c_sibling(u, self.half).start()
@@ -522,17 +587,18 @@
             self.c_sibling(u, self.other_half).wait_recv()
 
 
-def sum_scratch(units, slots):
+def sum_scratch(units, whole, slots):
+    pairs = (units - whole + 1) // 2
     return [
         pltpu.VMEM((slots, SPAN, WIDE), F32),
-        pltpu.VMEM((4, SPAN // 2, WIDE), F32),
-        pltpu.VMEM((4, SPAN // 4, WIDE), F32),
-        pltpu.VMEM((8, 3 * SPAN // 16, WIDE), F32),
-        pltpu.VMEM((8, 3 * SPAN // 16, WIDE), F32),
-        pltpu.VMEM((units, SPAN // 32, WIDE), F32),
+        pltpu.VMEM((2 + min(pairs, 2), SPAN // 2, WIDE), F32),
+        pltpu.VMEM((3 + min(pairs, 4), SPAN // 4, WIDE), F32),
+        pltpu.VMEM((3 + pairs, 5 * SPAN // 16, WIDE), F32),
+        pltpu.VMEM((whole + pairs, SPAN // 32, WIDE), F32),
         pltpu.SemaphoreType.DMA((KINDS, units)),
         pltpu.SemaphoreType.DMA((KINDS, units)),
         pltpu.SemaphoreType.DMA((units,)),
+        pltpu.SemaphoreType.REGULAR((4, units)),
     ]
 
 
@@ -609,35 +675,37 @@
         greeted = greeted + greet_ring(ring)
     small_v = own_v.at[0]
 
+    inner_columns = pl.ds(0, inner)
+    rest_columns = pl.ds(inner, w_in.shape[1] - inner)
     loads = [
         pltpu.make_async_copy(source, target, load_sems.at[k])
         for k, (source, target) in enumerate((
             (middle_in, middle_v), (w_up, w_up_v), (cot_in, cot_v), (w_down, w_down_v), (state_in, state_v),
-            (w_out, w_out_v), (w_in, w_in_v), (x_in, x_v),
+            (w_out, w_out_v), (x_in, x_v), (w_in.at[:, rest_columns], w_in_v), (w_in.at[:, inner_columns], w_up_v),
         ))
     ]
-    for load in loads:
-        load.start()
+    loads[0].start()
 
     def at_block(b, n=size):
         return pl.ds(pl.multiple_of(b * n, n), n)
 
-    flying = {}
-    waiting = []
-    clock = [0]
-
-    def pace(unit):
-        return SLOW if plan[unit][2] > UNIT else FAST
-
-    def tick():
-        now = clock[0]
-        clock[0] += 1
-        if waiting:
-            flying[waiting.pop(0)] = now
-        if ringed:
-            for unit in sorted(flying):
-                if now - flying[unit] in pace(unit):
-                    ring.stage(pace(unit).index(now - flying[unit]), unit)
+    due = {}
+    clock = [0.0]
+
+    def travel(unit, s):
+        return 2.0 * (SLOW[s] - SLOW[s - 1]) if plan[unit][2] == WIDE else 1.0 * (FAST[s] - FAST[s - 1])
+
+    def enter(unit):
+        due[unit] = (0, clock[0])
+
+    def tick(passed):
+        clock[0] += passed
+        for unit in sorted(due):
+            s, when = due[unit]
+            if s < STAGES and when <= clock[0] + 1e-6:
+                if ringed:
+                    ring.stage(s, unit)
+                due[unit] = (s + 1, clock[0] + travel(unit, s + 1) if s + 1 < STAGES else 0.0)
 
     def rolling_tick(i, half):
         for s in reversed(range(STAGES)):
@@ -645,11 +713,11 @@
             if ringed and behind % 2 == 0 and behind // 2 < feeds * per // 2:
                 pl.when(i >= behind // 2)(functools.partial(ring.stage, s, i - behind // 2))
 
-    def beat(number, body, ticks, *carry):
+    def beat(number, body, ticks, passed, *carry):
         each = number // ticks
         for k in range(ticks):
             carry = lax.fori_loop(each * k, each * k + each, lambda i, c: body(i, *c), carry)
-            tick()
+            tick(passed / ticks)
         return carry
 
     def put_unit(unit):
@@ -668,18 +736,12 @@
         for k in range(value.shape[1] // 128):
             small_v[pl.ds(row + k, 1)] = value[:, 128 * k : 128 * k + 128]
 
-    def gather(slot, column, value, fresh):
-        lanes = pl.ds(column, value.shape[1])
-
-        @pl.when(fresh)
-        def _():
-            grads[slot, :, lanes] = value
-
-        @pl.when(jnp.logical_not(fresh))
-        def _():
-            grads[slot, :, lanes] = grads[slot, :, lanes] + value
+    def gather(slot, value, fresh):
+        grads[slot] = jnp.where(fresh, 0.0, grads[slot]) + value
 
     loads[0].wait()
+    for k in (1, 2, 3):
+        loads[k].start()
     gains = gain_two[...]
     bias = down_bias[...]
 
@@ -697,6 +759,8 @@
     lax.fori_loop(0, blocks, norm_two, 0)
     for k in (1, 2, 3):
         loads[k].wait()
+    for k in (4, 5, 6, 7):
+        loads[k].start()
     pl.semaphore_wait(barrier, greeted)
 
     def feed(f, tok):
@@ -714,8 +778,8 @@
         act, back_up = act.astype(BF16), back_up.astype(BF16)
         mixed_v[at] = mixed_v[at] + dot(act, w_down_v[lanes])
         second_v[at] = second_v[at] + dot_nt(back_up, w_up_v[:, lanes])
-        gather(2 * f, 0, dot_tn(act, cot), tok == 0)
-        gather(2 * f + 1, 0, dot(turned_v[:, at], back_up), tok == 0)
+        gather(2 * f, dot_tn(act, cot), tok == 0)
+        gather(2 * f + 1, dot(turned_v[:, at], back_up), tok == 0)
 
     early = per - 1
 
@@ -732,9 +796,19 @@
         return carry
 
     lax.fori_loop(0, feeds * per // 2, feed_pair, 0)
-    clock[0] = feeds * per - early
-    flying.update({u: 2 * u for u in range(2 * feeds) if 2 * u < clock[0]})
-    waiting.extend(u for u in range(2 * feeds) if 2 * u >= clock[0])
+    clock[0] = 2.0 * (feeds * per - 1 - early)
+    for u in range(2 * feeds):
+        stages = [s for s in range(STAGES) if 4.0 * u + 2.0 * SLOW[s] > clock[0]]
+        due[u] = (stages[0], 4.0 * u + 2.0 * SLOW[stages[0]])
+
+    loads[8].start()
+
+    def decays(j):
+        slot = j % 2
+        return pltpu.make_async_copy(decay_in.at[:, pl.ds(j * wide, wide)], decay_s.at[slot], stream_sems.at[0, slot])
+
+    decays(0).start()
+    decays(1).start()
 
     def stage_copy(buffer, target, b):
         slot = lax.rem(b, 2)
@@ -761,7 +835,7 @@
         return norm_sum, cot_sum
 
     zero = jnp.zeros((8, width), F32)
-    norm_sum, cot_sum = beat(blocks, finish_two, 2, zero, zero)
+    norm_sum, cot_sum = beat(blocks, finish_two, 2, 2.4, zero, zero)
     for b in (blocks - 2, blocks - 1):
         stage_copy(mixed_s, mixed_out, b).wait()
     put_small(20, jnp.sum(norm_sum, axis=0, keepdims=True))
@@ -771,51 +845,55 @@
     loads[4].wait()
     loads[5].wait()
 
-    def stream(buffer, source, j, b, k):
-        slot = lax.rem(b, 2)
+    def stream(buffer, source, j, i, k):
+        slot = lax.rem(i, 4)
         lanes = pl.ds(j * wide, wide)
-        return pltpu.make_async_copy(source.at[at_block(b), lanes], buffer.at[slot], stream_sems.at[k, slot])
+        return pltpu.make_async_copy(source.at[at_block(blocks - 1 - i), lanes], buffer.at[slot], stream_sems.at[k, slot])
 
     def half_of(refs, j):
         return refs[j // 2], slice(UNIT * (j % 2), UNIT * (j % 2) + UNIT)
 
+    def back_states():
+        def one(tok, carry):
+            at = at_block(tok, big)
+            back = dot_nt(low_v[at], w_out_v[...])
+            mixed_v[at] = back[:, :SPAN]
+            middle_v[at] = back[:, SPAN:]
+            return carry
+
+        lax.fori_loop(0, per, one, 0)
+        tick(2.0)
+
     def first_pass(j):
         flows, lanes = half_of((mixed_v, middle_v), j)
-        stream(decay_s, decay_in, j, blocks - 1, 0).start()
-
-        def one(i, product, flow):
+        decays(j).wait()
+
+        def one(i, carry):
+            product, flow = carry
             b = blocks - 1 - i
-            at = at_block(b)
-
-            @pl.when(b > 0)
-            def _():
-                stream(decay_s, decay_in, j, b - 1, 0).start()
-            back = dot_nt(low_v[at], w_out_v[pl.ds(j * wide, wide)])
-            flows[at, lanes] = back
-            stream(decay_s, decay_in, j, b, 0).wait()
-            slot = lax.rem(b, 2)
             for t in reversed(range(block)):
-                here = slice(t * rows, (t + 1) * rows)
-                decay = decay_s[slot, here]
-                flow = decay * (back[here] + flow)
+                there = pl.ds(pl.multiple_of(b * size + t * rows, rows), rows)
+                decay = decay_s[j % 2, there]
+                flow = decay * (flows[there, lanes] + flow)
                 product = decay * product
             return product, flow
 
-        product, flow = lax.fori_loop(0, blocks, lambda i, c: one(i, *c), (jnp.ones((rows, wide), F32), jnp.zeros((rows, wide), F32)))
-        tick()
+        product, flow = lax.fori_loop(0, blocks, one, (jnp.ones((rows, wide), F32), jnp.zeros((rows, wide), F32)))
         chain.start(j, product, flow)
+        decays((j + 2) % parts).start()
+        tick(0.6)
 
     def grad_out():
         for j in range(hidden // SPAN):
             def one(tok, carry):
                 at = at_block(tok, big)
-                gather(2 * feeds + j, 0, dot_tn(state_v[at, pl.ds(j * SPAN, SPAN)], low_v[at]), tok == 0)
+                gather(2 * feeds + j, dot_tn(state_v[at, pl.ds(j * SPAN, SPAN)], low_v[at]), tok == 0)
                 return carry
 
             lax.fori_loop(0, per, one, 0)
             put_unit(2 * feeds + j)
-            waiting.append(2 * feeds + j)
-            tick()
+            enter(2 * feeds + j)
+            tick(2.0)
 
     gains_one = gain_one[...]
 
@@ -826,48 +904,60 @@
         turned_v[:, at] = jnp.swapaxes(value * scale * gains_one, 0, 1).astype(BF16)
         return ()
 
+    back_states()
     work = [functools.partial(first_pass, j) for j in range(parts)]
     work += [grad_out]
 
     def turn():
-        loads[7].wait()
-        beat(blocks, norm_one, 1)
+        loads[6].wait()
+        beat(blocks, norm_one, 1, 1.6)
 
     work.append(turn)
     for step in range(max(len(work), parts + chain.rounds)):
         if step < len(work):
             work[step]()
         else:
-            tick()
+            tick(1.0)
         for i in range(parts):
             if 0 <= step - 1 - i < chain.rounds:
                 chain.advance(i, step - 1 - i)
 
-    streams = ((decay_s, decay_in), (fade_s, fade_in), (rise_s, rise_in), (weight_s, weight_in), (lean_s, lean_in))
+    streams = ((fade_s, fade_in), (rise_s, rise_in), (weight_s, weight_in), (lean_s, lean_in))
+
+    def stream_all(j, i):
+        return [stream(buffer, source, j, i, 1 + k) for k, (buffer, source) in enumerate(streams)]
+
+    for i in range(3):
+        for copy in stream_all(0, i):
+            copy.start()
     cand_refs = (low_v, cand_v)
     input_refs = (cot_v, w_down_v)
 
     def second_pass(j):
         flows, lanes = half_of((mixed_v, middle_v), j)
         to_input, to_cand = half_of(input_refs, j)[0], half_of(cand_refs, j)[0]
-        for k, (buffer, source) in enumerate(streams):
-            stream(buffer, source, j, blocks - 1, k).start()
+        decays(j).wait()
 
         def one(i, flow, sum_f, sum_i):
             b = blocks - 1 - i
-            slot = lax.rem(b, 2)
-
-            @pl.when(b > 0)
+            slot = lax.rem(i, 4)
+
+            @pl.when(i + 3 < blocks)
             def _():
-                for k, (buffer, source) in enumerate(streams):
-                    stream(buffer, source, j, b - 1, k).start()
-            for k, (buffer, source) in enumerate(streams):
-                stream(buffer, source, j, b, k).wait()
+                for copy in stream_all(j, i + 3):
+                    copy.start()
+            if j + 1 < parts:
+                @pl.when(i + 3 >= blocks)
+                def _():
+                    for copy in stream_all(j + 1, i + 3 - blocks):
+                        copy.start()
+            for copy in stream_all(j, i):
+                copy.wait()
             for t in reversed(range(block)):
                 here = slice(t * rows, (t + 1) * rows)
                 there = pl.ds(pl.multiple_of(b * size + t * rows, rows), rows)
                 reach = flows[there, lanes] + flow
-                flow = decay_s[slot, here] * reach
+                flow = decay_s[j % 2, there] * reach
                 lean = reach * lean_s[slot, here].astype(F32)
                 grad_f = fade_s[slot, here].astype(F32) * lean
                 grad_i = -(rise_s[slot, here].astype(F32) * lean)
@@ -878,64 +968,78 @@
             return flow, sum_f, sum_i
 
         none = jnp.zeros((rows, wide), F32)
-        unused, sum_f, sum_i = beat(blocks, one, 2, join[j, 1], none, none)
+        unused, sum_f, sum_i = beat(blocks, one, 1, 1.2, join[j, 1], none, none)
+        if j + 2 < parts:
+            decays(j + 2).start()
         put_small(4 + 2 * j, jnp.sum(sum_f, axis=0, keepdims=True))
         put_small(12 + 2 * j, jnp.sum(sum_i, axis=0, keepdims=True))
 
     def grad_in(j):
         unit = 2 * feeds + hidden // SPAN + 3 * j
 
-        def one(tok, carry):
-            at = at_block(tok, big)
-            turned = turned_v[:, at]
-            lanes = half_of(input_refs, j)[1]
-            pieces = (state_v[at, wide * j : wide * j + wide], half_of(input_refs, j)[0][at, lanes], half_of(cand_refs, j)[0][at, lanes])
-            for k, piece in enumerate(pieces):
-                gather(*plan[unit + k][:2], dot(turned, piece), tok == 0)
-            return carry
-
-        lax.fori_loop(0, per, one, 0)
-        for k in range(3):
+        lanes = half_of(input_refs, j)[1]
+        pieces = ((state_v, slice(wide * j, wide * j + wide)), (half_of(input_refs, j)[0], lanes), (half_of(cand_refs, j)[0], lanes))
+        over = [u for u in range(2 * feeds + hidden // SPAN) if plan[u][0] in {plan[unit + k][0] for k in range(3)} and u not in settled]
+        settled.update(over)
+        assert all(due[u][0] > 7 for u in over)
+        if ringed and over:
+            ring.settle_sums(over)
+        for k, (ref, columns) in enumerate(pieces):
+            slot, column, length = plan[unit + k]
+            grads[slot, :, pl.ds(column, length)] = dot(turned_v[...], ref[:, columns])
             put_unit(unit + k)
-            waiting.append(unit + k)
-        tick()
-
+            enter(unit + k)
+            tick(0.5)
+
+    settled = set()
     for j in range(parts):
         second_pass(j)
         grad_in(j)
 
-    loads[6].wait()
-
-    def finish_one(b, norm_sum):
-        at = at_block(b)
-
-        @pl.when(b >= 2)
-        def _():
-            stage_copy(tokens_s, tokens_out, b - 2).wait()
-        grad = dot_nt(state_v[at], w_in_v[:, :hidden])
-        for k, refs in enumerate((input_refs, cand_refs)):
-            for half in range(2):
-                columns = pl.ds((k + 1) * hidden + half * SPAN, SPAN)
-                grad = grad + dot_nt(refs[half][at], w_in_v[:, columns])
-        value = x_v[at].astype(F32)
-        scale = lax.rsqrt(jnp.mean(value * value, axis=-1, keepdims=True) + EPS)
-        plain = value * scale
-        norm_sum = norm_sum + jnp.sum((grad * plain).reshape(size // 8, 8, width), axis=0)
-        lean = grad * gains_one
-        back = second_v[at] + scale * (lean - plain * jnp.mean(lean * plain, axis=-1, keepdims=True))
-        tokens_s[lax.rem(b, 2)] = jnp.swapaxes(back.reshape(block, rows, width), 0, 1)
-        stage_copy(tokens_s, tokens_out, b).start()
+    for k in (7, 8):
+        loads[k].wait()
+    project_refs = [(state_v, slice(0, hidden), w_up_v, 0)]
+    for k, refs in enumerate((input_refs, cand_refs)):
+        for half in range(2):
+            column = (k + 1) * hidden + half * SPAN
+            wide_ref, column = (w_up_v, column) if column < inner else (w_in_v, column - inner)
+            project_refs.append((refs[half], slice(None), wide_ref, column))
+
+    def finish_one(tok, norm_sum):
+        at = at_block(tok, big)
+        grad_all = jnp.zeros((big, width), F32)
+        for ref, columns, weight, column in project_refs:
+            piece = ref[at, columns]
+            grad_all = grad_all + dot_nt(piece, weight[:, column : column + piece.shape[1]])
+        for k in range(big // size):
+            b = tok * (big // size) + k
+
+            @pl.when(b >= 2)
+            def _():
+                stage_copy(tokens_s, tokens_out, b - 2).wait()
+            here = at_block(b)
+            grad = grad_all[k * size : k * size + size]
+            value = x_v[here].astype(F32)
+            scale = lax.rsqrt(jnp.mean(value * value, axis=-1, keepdims=True) + EPS)
+            plain = value * scale
+            norm_sum = norm_sum + jnp.sum((grad * plain).reshape(size // 8, 8, width), axis=0)
+            lean = grad * gains_one
+            back = second_v[here] + scale * (lean - plain * jnp.mean(lean * plain, axis=-1, keepdims=True))
+            tokens_s[lax.rem(b, 2)] = jnp.swapaxes(back.reshape(block, rows, width), 0, 1)
+            stage_copy(tokens_s, tokens_out, b).start()
         return (norm_sum,)
 
-    (norm_sum,) = beat(blocks, finish_one, 8, jnp.zeros((8, width), F32))
+    (norm_sum,) = beat(per, finish_one, 4, 9.0, jnp.zeros((8, width), F32))
     put_small(0, jnp.sum(norm_sum, axis=0, keepdims=True))
     if ringed:
         step = 0
-        while step <= DOUBLINGS or waiting or any(clock[0] <= flying[unit] + pace(unit)[-1] for unit in flying):
-            tick()
+        while step <= DOUBLINGS or any(due[unit][0] < STAGES for unit in due):
+            tick(1.0)
             if step <= DOUBLINGS:
                 small.step(step)
             step += 1
+        ring.settle_sums([u for u in due if u not in settled])
+        ring.settle_lines(list(due))
         copy = pltpu.make_async_copy(own_v.at[DOUBLINGS], small_out.at[0], load_sems.at[0])
     else:
         copy = pltpu.make_async_copy(small_v, small_out.at[0], load_sems.at[0])
@@ -960,15 +1064,14 @@
     feeds = inner // SPAN
     whole = 2 * feeds + hidden // SPAN
     plan = [(u, 0, WIDE) for u in range(whole)]
-    for j in range(parts):
-        slot = (whole + 2 * j) % SLOTS
-        plan += [(slot, 0, UNIT), (slot, UNIT, UNIT), (slot + 1, 0, UNIT)]
+    for k in range(3 * parts):
+        plan.append(((whole + k // 2) % SLOTS, k % 2 * UNIT, UNIT))
     units = len(plan)
     anywhere = pl.BlockSpec(memory_space=pl.ANY)
     vmem = pl.BlockSpec(memory_space=pltpu.VMEM)
     shape = jax.ShapeDtypeStruct
     if ringed:
-        first, *others = sum_scratch(units, SLOTS)
+        first, *others = sum_scratch(units, whole, SLOTS)
         more = [first, pltpu.VMEM((DOUBLINGS + 1, SMALL_ROWS, 128), F32), *others]
         more += [pltpu.VMEM((DOUBLINGS, SMALL_ROWS, 128), F32)] + [pltpu.SemaphoreType.DMA((DOUBLINGS,))] * 2
     else:
@@ -984,15 +1087,15 @@
             pltpu.VMEM((total, width), F32), pltpu.VMEM((total, width), F32), pltpu.VMEM((total, width), F32),
             pltpu.VMEM((total, hidden), BF16), pltpu.VMEM((total, width), BF16), pltpu.VMEM((total, width), BF16), pltpu.VMEM((total, width), BF16),
             pltpu.VMEM((total, width), BF16), pltpu.VMEM((width, total), BF16),
-            pltpu.VMEM(w_in.shape, BF16), pltpu.VMEM(w_out.shape, BF16), pltpu.VMEM(w_up.shape, BF16), pltpu.VMEM(w_down.shape, BF16),
-            pltpu.VMEM((2, size, wide), F32), pltpu.VMEM((2, size, wide), BF16), pltpu.VMEM((2, size, wide), BF16),
-            pltpu.VMEM((2, size, wide), BF16), pltpu.VMEM((2, size, wide), BF16),
+            pltpu.VMEM((width, w_in.shape[1] - inner), BF16), pltpu.VMEM(w_out.shape, BF16), pltpu.VMEM(w_up.shape, BF16), pltpu.VMEM(w_down.shape, BF16),
+            pltpu.VMEM((2, total, wide), F32), pltpu.VMEM((4, size, wide), BF16), pltpu.VMEM((4, size, wide), BF16),
+            pltpu.VMEM((4, size, wide), BF16), pltpu.VMEM((4, size, wide), BF16),
             pltpu.VMEM((2, rows, block, width), BF16), pltpu.VMEM((2, rows, block, width), F32), pltpu.VMEM((8, inner), F32),
-            pltpu.SemaphoreType.DMA((8,)), pltpu.SemaphoreType.DMA((5, 2)), pltpu.SemaphoreType.DMA((2,)),
+            pltpu.SemaphoreType.DMA((9,)), pltpu.SemaphoreType.DMA((5, 4)), pltpu.SemaphoreType.DMA((2,)),
             *chain_scratch(parts, count, rows, wide),
             *more,
         ],
-        compiler_params=pltpu.CompilerParams(collective_id=cid, has_side_effects=True, vmem_limit_bytes=63 * 2**20),
+        compiler_params=pltpu.CompilerParams(collective_id=cid, has_side_effects=True, vmem_limit_bytes=63 * 2**20 + 2**19),
         cost_estimate=pl.CostEstimate(flops=2 * total * width * (8 * hidden + 6 * inner), bytes_accessed=80 * 2**20, transcendentals=total * inner),
         name="back",
     )(x, cot, middle, state, decay, fade, rise, weight, lean, gain_one.reshape(1, -1), gain_two.reshape(1, -1), up_bias.reshape(1, -1), down_bias.reshape(1, -1), w_in, w_out, w_up, w_down)

time: 271 us -> 250 us (0.923)
  Pallas kernels: 266 us -> 244 us
    pallas_call x1, Pallas kernels: 214 us -> 201 us  [back(): pl.pallas_call(functools.partial(back_kernel, ringed, count, rows, steps,...]
    pallas_call x1, Pallas kernels: 35.4 us -> 27.6 us  [front(): pl.pallas_call(functools.partial(front_kernel, count, rows, steps, chunk,...]
where the time goes in v4:
time: 250 us; the launch traced here: 249 us
  Pallas kernels  244 us (98%)
  local copies, waits for them, and re-layouts  3.68 us (1%)
    pallas_call x1, Pallas kernels, back(): pl.pallas_call(functools.partial(back_kernel, ringed, count, rows, steps,...  201 us
    pallas_call x1, Pallas kernels, front(): pl.pallas_call(functools.partial(front_kernel, count, rows, steps, chunk,...  27.6 us
    pallas_call x1, Pallas kernels, settle(): pl.pallas_call(functools.partial(settle_kernel, places), out_shape=(shape...  16.3 us

profile of v4, /device:TPU:0, one launch (start us, length us, event | category | flops | bytes accessed | tf_op | source)
XLA Modules:
  0.0 249.0 jit_solution(2308173340527342282)
XLA Ops:
  0.6 1.4 copy.25.reset
  2.0 27.6 %front.1 = (bf16[2048,512]{1,0:T(8,128)(2,1)}, bf16[2048,512]{1,0:T(8,128)(2,1)}, f32[2048,512]{1,0:T(8,128)}, bf16[2048,1024]{1,0:T(8,128)(2,1)}, f32[2048,1024...) custom-call(bf16[16,128,512]{2,1,0:T(8,128)(2,1)} %tokens.1, ...), custom_call_target="tpu_custom_call" | custom-call | flops 8589934592 | bytes 41943040 | tf_op jit(solution)/shard_map/front/pallas_call | solution.py:320
  29.6 200.6 %back.1 = (bf16[16,128,512]{2,1,0:T(8,128)(2,1)}, f32[16,128,512]{2,1,0:T(8,128)}, f32[22,512,512]{2,1,0:T(8,128)}, f32[1,48,128]{2,1,0:T(8,128)}) custom-call(bf16[2048,512]{1,0:T(8,128)(2,1)} %get-tuple-element.37.x_in, bf16[2048,512]{1,0:T(8,128)(2,1)} %get-tuple-element.38.cot_in, f32[2048,512]{1,0:T(8,128)} %get-tuple-element.39.middle_in, ...), custom_call_target="tpu_custom_call" | custom-call | flops 42949672960 | bytes 83886080 | tf_op jit(solution)/shard_map/back/pallas_call | solution.py:1079
  230.2 0.0 copy-start
  230.2 1.6 copy-done
  231.8 0.0 copy-start.1
  231.8 0.7 copy-done.1
  232.5 16.3 %settle.1 = (bf16[16,128,512]{2,1,0:T(8,128)(2,1)}, f32[16,128,512]{2,1,0:T(8,128)}, f32[512,3072]{1,0:T(8,128)}, f32[1024,512]{1,0:T(8,128)}, f32[512,2048]{1,0...) custom-call(bf16[16,128,512]{2,1,0:T(8,128)(2,1)S(1)} %copy-done, ...), custom_call_target="tpu_custom_call" | custom-call | tf_op jit(solution)/shard_map/settle/pallas_call | solution.py:1144
Async XLA Ops:
  230.2 1.6 copy-start
  231.8 0.7 copy-start.1
